TPU v7x, 128 devices: a whole 4x4x4 slice. The times are simulated.
128 devices in a mesh: dp: 128 (over z, x, y, core).
Axes of the slice: x: 4, y: 4, z: 4, core: 2. Of those that a mesh axis runs over, the one named last changes fastest.
Arguments:
- queries: bfloat16 [65536, 1024], P('dp'), may hold values from -6 to 6
- resp_kv: bfloat16 [65536, 256], P('dp'), may hold values from -6 to 6
- prefix_kv: bfloat16 [8192, 256], P('dp'), may hold values from -6 to 6
- grad_out: bfloat16 [65536, 1024], P('dp'), may hold values from -6 to 6
- held_block: int32 [128], replicated, may hold values from 0 to 127, each once
- resp_prompt: int32 [128], replicated, may hold values from 0 to 3, as said below
- resp_len: int32 [128], replicated, may hold values from 64 to 512
Outputs:
- attn_out: bfloat16 [65536, 1024], P('dp')
- grad_q: bfloat16 [65536, 1024], P('dp')
- grad_resp_kv: bfloat16 [65536, 256], P('dp')
- grad_prefix_kv: float32 [8192, 256], P('dp')
Inputs may be any that keep to these rules, and one draw needn't show every extreme that they name: `resp_prompt`: each prompt is named by exactly 32 devices.
All inputs are finite; a program needn't handle non-finite values.
Results may differ from a plain program's by a relative error of at most 0.0095.
Values may be sent and summed in bfloat16 or wider, within the bound.
A program may use at most 64 MiB of HBM per device.

v0:
```python
import jax
import jax.numpy as jnp
from jax import lax
from jax.sharding import PartitionSpec as P

PROMPT_LEN = 2048


def attend(queries, key_rows, value_rows, grad_out, length, score_scale):
    row_count = queries.shape[0]
    head_width = key_rows.shape[1]
    head_count = queries.shape[1] // head_width
    key_count = key_rows.shape[0]
    prompt_rows = key_count - row_count
    head_group = max(1, min(head_count, 512 // row_count))
    while head_count % head_group != 0:
        head_group = head_group - 1
    block_count = head_count // head_group
    stacked = head_group * row_count
    live_rows = jnp.arange(row_count) < length
    masked = jnp.where(live_rows[:, None], grad_out, jnp.zeros((), grad_out.dtype))
    query_stack = (
        queries.reshape(row_count, block_count, head_group, head_width)
        .transpose(1, 2, 0, 3)
        .reshape(block_count, stacked, head_width)
    )
    grad_stack = (
        masked.reshape(row_count, block_count, head_group, head_width)
        .transpose(1, 2, 0, 3)
        .reshape(block_count, stacked, head_width)
    )
    position = jnp.tile(jnp.arange(row_count), head_group)
    column = jnp.arange(key_count)
    allowed = (column[None, :] < prompt_rows) | (column[None, :] - prompt_rows <= position[:, None])
    valid_rows = jnp.tile(live_rows, head_group)[:, None]

    def one_block(totals, inputs):
        key_grad, value_grad = totals
        query_block, grad_block = inputs
        scores = jnp.dot(query_block, key_rows.T, preferred_element_type=jnp.float32) * score_scale
        scores = jnp.where(allowed, scores, jnp.float32(-1e30))
        row_max = jnp.max(scores, axis=1, keepdims=True)
        exponent = jnp.exp(scores - row_max)
        weights = exponent / jnp.sum(exponent, axis=1, keepdims=True)
        weight_short = weights.astype(jnp.bfloat16)
        output = jnp.where(
            valid_rows,
            jnp.dot(weight_short, value_rows, preferred_element_type=jnp.float32),
            jnp.float32(0.0),
        )
        weight_grad = jnp.dot(grad_block, value_rows.T, preferred_element_type=jnp.float32)
        row_delta = jnp.sum(grad_block.astype(jnp.float32) * output, axis=1, keepdims=True)
        score_grad = weights * (weight_grad - row_delta)
        score_short = score_grad.astype(jnp.bfloat16)
        query_grad = (
            jnp.dot(score_short, key_rows, preferred_element_type=jnp.float32) * score_scale
        )
        key_grad = (
            key_grad
            + jnp.dot(score_short.T, query_block, preferred_element_type=jnp.float32) * score_scale
        )
        value_grad = value_grad + jnp.dot(
            weight_short.T, grad_block, preferred_element_type=jnp.float32
        )
        return (
            (key_grad, value_grad),
            (output.astype(jnp.bfloat16), query_grad.astype(jnp.bfloat16)),
        )

    start = (
        jnp.zeros((key_count, head_width), jnp.float32),
        jnp.zeros((key_count, head_width), jnp.float32),
    )
    (key_grad, value_grad), (output, query_grad) = lax.scan(
        one_block, start, (query_stack, grad_stack)
    )
    output = (
        output.reshape(block_count, head_group, row_count, head_width)
        .transpose(2, 0, 1, 3)
        .reshape(row_count, head_count * head_width)
    )
    query_grad = (
        query_grad.reshape(block_count, head_group, row_count, head_width)
        .transpose(2, 0, 1, 3)
        .reshape(row_count, head_count * head_width)
    )
    resp_grad = jnp.concatenate([key_grad[prompt_rows:], value_grad[prompt_rows:]], axis=1).astype(
        jnp.bfloat16
    )
    pref_grad = jnp.concatenate([key_grad[:prompt_rows], value_grad[:prompt_rows]], axis=1)
    return (output, query_grad, resp_grad, pref_grad)


def on_device(queries, resp_kv, prefix_kv, grad_out, held_block, resp_prompt, resp_len):
    myself = lax.axis_index("dp")
    block_rows = prefix_kv.shape[0]
    pair_width = prefix_kv.shape[1]
    head_width = pair_width // 2
    blocks_per = PROMPT_LEN // block_rows
    score_scale = 1.0 / head_width**0.5
    prompt = resp_prompt[myself]
    length = resp_len[myself]
    blank = jnp.zeros((PROMPT_LEN, pair_width), jnp.bfloat16)
    piece = lax.all_gather(prefix_kv, "dp", axis=0, tiled=True)
    spots = jnp.arange(piece.shape[0], dtype=jnp.int32)
    block = held_block[spots // block_rows]
    where_to = block % blocks_per * block_rows + spots % block_rows
    where_to = jnp.where(block // blocks_per == prompt, where_to, PROMPT_LEN)
    prefix = blank.at[where_to].set(piece, mode="drop")
    joined = jnp.concatenate([prefix, resp_kv], axis=0)
    output, query_grad, resp_grad, pref_grad = attend(
        queries, joined[:, :head_width], joined[:, head_width:], grad_out, length, score_scale
    )
    spots = jnp.arange(block_rows * lax.axis_size("dp"), dtype=jnp.int32)
    block = held_block[spots // block_rows]
    matches = block // blocks_per == prompt
    source = jnp.where(matches, block % blocks_per * block_rows + spots % block_rows, 0)
    gathered_grad = lax.psum_scatter(
        jnp.where(matches[:, None], pref_grad[source], jnp.float32(0.0)),
        "dp",
        scatter_dimension=0,
        tiled=True,
    )
    return (output, query_grad, resp_grad, gathered_grad)


def solution(mesh):
    placed = (P("dp", None), P("dp", None), P("dp", None), P("dp", None), P(), P(), P())
    return jax.shard_map(
        on_device,
        mesh=mesh,
        in_specs=placed,
        out_specs=(P("dp", None), P("dp", None), P("dp", None), P("dp", None)),
        check_vma=False,
    )
```

profile of v0, /device:TPU:0, one launch (start us, length us, event | category | flops | bytes accessed | tf_op | source)
XLA Modules:
  0.0 945.1 jit_solution(13268225290328838831)
XLA Ops:
  8.0 1.2 dynamic_slice.14
  9.3 1.2 dynamic_slice.13
  11.1 2.4 broadcast_select_fusion.1
  13.5 2.3 copy.16
  15.8 2.3 copy.15
  18.1 48.9 %gather_fusion = s32[8192]{0:T(1024)S(1)} fusion(s32[128]{0:T(128)S(1)} %copy-done, s32[8192]{0:T(1024)S(1)} %broadcast_clamp_fusion.1), kind=kCustom, calls=%fused_computation | custom fusion | bytes 98304 | tf_op jit(solution)/shard_map/gather | solution.py:106
  69.4 11.1 %all-gather.2.cloned.1.call-done = bf16[8192,256]{1,0:T(8,128)(2,1)} async-done(((bf16[64,256]{1,0:T(8,128)(2,1)}), bf16[8192,256]{1,0:T(8,128)(2,1)}) %all-gather.2.cloned.1.call-update) | async-done | bytes 4194320 | tf_op jit(solution)/shard_map/all_gather | solution.py:104
  80.5 36.2 %scatter_custom_fusion = bf16[2048,256]{1,0:T(8,128)(2,1)} fusion(s32[8192]{0:T(1024)S(1)} %bitcast.93, bf16[8192,256]{1,0:T(8,128)(2,1)} %all-gather.2.cloned.1.call-done, bf16[]{:T(256)} %constant.92.clone.1), kind=kCustom, calls=%fused_computation.42 | custom fusion | bytes 1049088 | tf_op jit(solution)/shard_map/scatter | solution.py:109
  116.7 1.3 constant_dynamic-update-slice_fusion.1
  119.0 130.7 %while.17 = (s32[]{:T(128)}, f32[2560,128]{1,0:T(8,128)S(1)}, f32[2560,128]{1,0:T(8,128)S(1)}, bf16[8,512,128]{1,2,0:T(8,128)(2,1)}, bf16[8,512,128]{2,1,0:T(8,1...) while((s32[]{:T(128)}, f32[2560,128]{1,0:T(8,128)S(1)}, ...), condition=%wide.region_5.6_spmd.clone, body=%wide.region_1.5_spmd.clone.sunk | while | flops 2033712128 | bytes 56258256 | solution.py:74
  119.6 2.9 fusion.70
  124.5 1.9 multiply_reduce_fusion.2
  127.1 2.4 convolution_add_fusion.2
  129.6 2.0 multiply_convert_fusion.2
  131.6 1.5 fusion.74
  133.1 2.2 fusion.73
  135.9 2.9 fusion.70
  140.8 1.9 multiply_reduce_fusion.2
  143.5 2.4 convolution_add_fusion.2
  145.9 2.0 multiply_convert_fusion.2
  147.9 1.5 fusion.74
  149.4 2.2 fusion.73
  152.3 2.9 fusion.70
  157.2 1.9 multiply_reduce_fusion.2
  159.8 2.4 convolution_add_fusion.2
  162.3 2.0 multiply_convert_fusion.2
  164.2 1.5 fusion.74
  165.8 2.2 fusion.73
  168.6 2.9 fusion.70
  172.3 1.2 fusion.72
  173.5 1.9 multiply_reduce_fusion.2
  176.2 2.4 convolution_add_fusion.2
  178.6 2.0 multiply_convert_fusion.2
  180.6 1.5 fusion.74
  182.1 2.2 fusion.73
  185.0 2.9 fusion.70
  189.9 1.9 multiply_reduce_fusion.2
  192.5 2.4 convolution_add_fusion.2
  194.9 2.0 multiply_convert_fusion.2
  196.9 1.5 fusion.74
  198.4 2.2 fusion.73
  201.3 2.9 fusion.70
  206.2 1.9 multiply_reduce_fusion.2
  208.8 2.4 convolution_add_fusion.2
  211.3 2.0 multiply_convert_fusion.2
  213.3 1.5 fusion.74
  214.8 2.2 fusion.73
  217.7 2.9 fusion.70
  222.6 1.9 multiply_reduce_fusion.2
  225.2 2.4 convolution_add_fusion.2
  227.6 2.0 multiply_convert_fusion.2
  229.6 1.5 fusion.74
  231.1 2.2 fusion.73
  234.0 2.9 fusion.70
  238.9 1.9 multiply_reduce_fusion.2
  241.5 2.4 convolution_add_fusion.2
  244.0 2.0 multiply_convert_fusion.2
  246.0 1.5 fusion.74
  247.5 2.2 fusion.73
  251.1 31.6 %gather_fusion.1 = f32[8192,256]{1,0:T(8,128)} fusion(f32[2048,256]{1,0:T(8,128)S(1)} %pad_maximum_fusion, s32[8192]{0:T(1024)S(1)} %broadcast_clamp_fusion), kind=kCustom, calls=%fused_computation.1 | custom fusion | bytes 16809984 | tf_op jit(solution)/shard_map/gather | solution.py:119
  282.7 7.4 broadcast_select_fusion
  292.1 1.2 copy.25
  293.3 1.3 copy.21
  295.4 642.9 %reduce-scatter.2.cloned.1.call-done = f32[64,256]{1,0:T(8,128)} async-done(((f32[8192,256]{1,0:T(8,128)}), f32[64,256]{1,0:T(8,128)}) %reduce-scatter.2.cloned.1.call-update) | async-done | bytes 65552 | tf_op jit(solution)/shard_map/reduce_scatter | solution.py:118
  (83 shorter events, 34.2 us)
Async XLA Ops:
  7.2 10.9 %copy-start = (s32[128]{0:T(128)S(1)}, s32[128]{0:T(128)}, u32[]{:S(2)}) copy-start(s32[128]{0:T(128)} %param.13) | copy-start | bytes 1540
  7.2 73.3 %all-gather.2.cloned.1.call-start = ((), (), s32[]{:S(2)}) async-start(), calls=%async_computation.1 | async-start | bytes 4227072 | tf_op jit(solution)/shard_map/all_gather | solution.py:104
  7.9 930.3 %reduce-scatter.2.cloned.1.call-start = ((), (), s32[]{:S(2)}) async-start(), calls=%async_computation.2 | async-start | bytes 8454144 | tf_op jit(solution)/shard_map/reduce_scatter | solution.py:118
  67.0 51.0 %copy-start.5 = (bf16[512,256]{1,0:T(8,128)(2,1)S(1)}, bf16[512,256]{1,0:T(8,128)(2,1)}, u32[]{:S(2)}) copy-start(bf16[512,256]{1,0:T(8,128)(2,1)} %param.10) | copy-start | bytes 786436
  129.6 2.0 copy-start.4
  145.9 2.0 copy-start.4
  162.2 2.0 copy-start.4
  178.6 2.0 copy-start.4
  194.9 2.0 copy-start.4
  211.3 2.0 copy-start.4
  227.6 2.0 copy-start.4
  244.0 2.0 copy-start.4
  249.7 1.2 copy-start.1
  290.1 1.3 copy-start.2
  290.1 3.2 copy-start.3
Sparse Core Ops, SparseCore 0:
  11.1 69.2 all-gather.1
  290.2 647.9 reduce-scatter.1
where the time goes:
time: 946 us; the launch traced here: 945 us
  waiting for transfers between devices  655 us (69%)
  local copies, waits for them, and re-layouts  137 us (14%)
  matrix products  104 us (11%)
  other arithmetic  34.9 us (4%)
  between operations  14.2 us (2%)
    reduce_scatter x1, waiting for transfers between devices, on_device(): lax.psum_scatter(jnp.where(matches[:, None], pref_grad[source], jnp.float...  643 us
    gather x1, local copies, waits for them, and re-layouts, on_device(): block = held_block[spots // block_rows]  48.9 us
    scatter x1, local copies, waits for them, and re-layouts, on_device(): prefix = blank.at[where_to].set(piece, mode='drop')  36.2 us
    gather x1, local copies, waits for them, and re-layouts, on_device(): pref_grad[source]  31.6 us
    dot_general x8, matrix products, one_block(): jnp.dot(query_block, key_rows.T, preferred_element_type=jnp.float32)  22.8 us
    dot_general x8, matrix products, one_block(): jnp.dot(weight_short.T, grad_block, preferred_element_type=jnp.float32)  19.4 us
  transfers between devices with their start and end apart: 2, of which 2 were waited for; matrix products, arithmetic and copies ran while one was open for 7% of the time, Pallas kernels for 0%

commit v1 on v0

v1 whole, which is shorter than its diff:
```python
import functools
import math

import jax
import jax.numpy as jnp
from jax import lax
from jax.experimental import pallas as pl
from jax.experimental.pallas import tpu as pltpu
from jax.sharding import PartitionSpec as P

f32, bf16 = jnp.float32, jnp.bfloat16
NN = (((1,), (0,)), ((), ()))
NT = (((1,), (1,)), ((), ()))


def mm(a, b, dims=NN):
    return lax.dot_general(a, b, dims, preferred_element_type=f32)


def attend(length, q_ref, g_ref, rkv_ref, pkv_ref, o_ref, dq_ref, drkv_ref, dpkv_ref,
                kk, vv, kt, vt, s_scr, e_scr, dk, dv):
    rows, width = q_ref.shape
    d = 128
    heads = width // d
    np_ = pkv_ref.shape[0]
    nk = np_ + rows
    scale = 1.0 / math.sqrt(d)
    c = scale * math.log2(math.e)
    kk[0:np_, 0:d] = pkv_ref[:, 0:d]
    kk[0:np_, d:] = pkv_ref[:, 0:d]
    kk[np_:, 0:d] = rkv_ref[:, 0:d]
    kk[np_:, d:] = rkv_ref[:, 0:d]
    vv[0:np_, 0:d] = pkv_ref[:, d:]
    vv[np_:, 0:d] = rkv_ref[:, d:]
    vv[:, d:] = jnp.ones((nk, d), bf16)
    for i in range(0, nk, 512):
        kt[:, i:i + 512] = kk[i:i + 512, 0:d].T
        vt[:, i:i + 512] = vv[i:i + 512, 0:d].T
    dk[...] = jnp.zeros_like(dk)
    dv[...] = jnp.zeros_like(dv)
    live = lax.broadcasted_iota(jnp.int32, (1, rows), 1) < length
    half = rows // 2
    chunks = [(i, 512, 0) for i in range(0, np_, 512)] + [(np_, half, 0), (np_ + half, half, half)]
    tri = (lax.broadcasted_iota(jnp.int32, (half, half), 0)
           <= lax.broadcasted_iota(jnp.int32, (half, half), 1))

    def head(h, _):
        hs = pl.ds(pl.multiple_of(h * d, d), d)
        q = q_ref[:, hs]
        qs = q.astype(f32) * c
        qhi = qs.astype(bf16)
        qlo = (qs - qhi.astype(f32)).astype(bf16)
        q2t = jnp.concatenate([qhi, qlo], axis=1).T
        m = jnp.full((1, rows), -jnp.inf, f32)
        for k0, kn, r0 in chunks:
            s = mm(kk[k0:k0 + kn, :], q2t[:, r0:])
            if k0 >= np_:
                diag = jnp.where(tri, s[:, 0:half], -1e30)
                s = diag if r0 else jnp.concatenate([diag, s[:, half:]], axis=1)
            s_scr[k0:k0 + kn, r0:] = s
            cm = jnp.max(s, axis=0, keepdims=True)
            if r0:
                cm = jnp.concatenate([m[:, :r0], jnp.maximum(m[:, r0:], cm)], axis=1)
                m = cm
            else:
                m = jnp.maximum(m, cm)
        l = jnp.zeros((1, rows), f32)
        ot = jnp.zeros((d, rows), f32)
        for k0, kn, r0 in chunks:
            e = jnp.exp2(s_scr[k0:k0 + kn, r0:] - m[:, r0:])
            cl = jnp.sum(e, axis=0, keepdims=True)
            eb = e.astype(bf16)
            e_scr[k0:k0 + kn, r0:] = eb
            co = mm(vt[:, k0:k0 + kn], eb)
            if r0:
                l = jnp.concatenate([l[:, :r0], l[:, r0:] + cl], axis=1)
                ot = jnp.concatenate([ot[:, :r0], ot[:, r0:] + co], axis=1)
            else:
                l = l + cl
                ot = ot + co
        f = jnp.where(live, 1.0 / l, 0.0)
        ot = ot * f
        o_ref[:, hs] = ot.astype(bf16).T
        gt = g_ref[:, hs].T.astype(f32)
        gt = jnp.where(live, gt, 0.0)
        gpt = gt * f
        ndelta = -jnp.sum(gpt * ot, axis=0, keepdims=True)
        gptb = gpt.astype(bf16)
        gp = gptb.T
        dhi = ndelta.astype(bf16)
        dlo = (ndelta - dhi.astype(f32)).astype(bf16)
        sub = lax.broadcasted_iota(jnp.int32, (16, rows), 0)
        extra = jnp.where(sub == 0, dhi.astype(f32), jnp.where(sub == 1, dlo.astype(f32), 0.0)).astype(bf16)
        g2t = jnp.concatenate([gptb, extra, jnp.zeros((d - 16, rows), bf16)], axis=0)
        dqt = jnp.zeros((d, rows), f32)
        for k0, kn, r0 in chunks:
            dp = mm(vv[k0:k0 + kn, :], g2t[:, r0:])
            eb = e_scr[k0:k0 + kn, r0:]
            ds = eb * dp.astype(bf16)
            cq = mm(kt[:, k0:k0 + kn], ds)
            if r0:
                dqt = jnp.concatenate([dqt[:, :r0], dqt[:, r0:] + cq], axis=1)
            else:
                dqt = dqt + cq
            dk[k0:k0 + kn, :] += mm(ds, q[r0:, :])
            dv[k0:k0 + kn, :] += mm(eb, gp[r0:, :])
        dq_ref[:, hs] = (dqt * scale).astype(bf16).T
        return 0

    lax.fori_loop(0, heads, head, 0)
    nb = np_ // 64
    drkv_ref[:, 0:d] = (dk[np_:, :] * scale).astype(bf16)
    drkv_ref[:, d:] = dv[np_:, :].astype(bf16)
    dpkv_ref[:, 0:64, :] = (dk[0:np_, :] * scale).astype(bf16).reshape(nb, 64, d)
    dpkv_ref[:, 64:, :] = dv[0:np_, :].astype(bf16).reshape(nb, 64, d)


MESH = pl.DeviceIdType.MESH
SIDE = 4


def place():
    me = lax.axis_index("dp")
    return (me // 32, me // 8 % 4, me // 2 % 4), me % 2


def device(at, core):
    return ((at[0] * SIDE + at[1]) * SIDE + at[2]) * 2 + core


def moved(at, axis, step):
    return tuple((c + step + SIDE) % SIDE if a == axis else c for a, c in enumerate(at))


def enter(at, core):
    barrier = pltpu.get_barrier_semaphore()
    near = [device(moved(at, a, s), core) for a in range(3) for s in (1, -1)] + [device(at, 1 - core)]
    for n in near:
        pl.semaphore_signal(barrier, inc=1, device_id=(n,), device_id_type=MESH)
    pl.semaphore_wait(barrier, len(near))


class Sender:
    def __init__(self, send, recv):
        self.send, self.recv, self.count, self.all = send, recv, 0, []

    def __call__(self, src, dst, to):
        i = self.count
        self.count += 1
        c = pltpu.make_async_remote_copy(src_ref=src, dst_ref=dst, send_sem=self.send.at[i], recv_sem=self.recv.at[i],
                                         device_id=(to,), device_id_type=MESH)
        c.start()
        self.all.append(c)
        return c

    def drain(self):
        for c in self.all:
            c.wait_send()


AG_PARTS = [((0, 48), (0, 128), (0, 1, 2)), ((0, 48), (128, 256), (1, 2, 0)), ((48, 64), (0, 256), (2, 0, 1))]


def gather(go, loc_ref, prompt, x_ref, out_ref, g):
    at, core = place()
    sib = device(at, 1 - core)
    g[at[0], at[1], at[2], core] = x_ref[...]

    def view(part, idx):
        (r0, r1), (c0, c1), _ = part
        return g.at[idx[0], idx[1], idx[2], core, r0:r1, c0:c1]

    def block(order, i, k, half=None):
        idx = []
        for a in range(3):
            if a in order[:i]:
                if half is not None and a == order[0]:
                    idx.append(slice(2 * half, 2 * half + 2))
                else:
                    idx.append(slice(0, SIDE))
            elif a == order[i]:
                idx.append(k)
            else:
                idx.append(at[a])
        return idx

    def half_view(part, i, k, half):
        (r0, r1), (c0, c1), order = part
        if i > 0:
            return view(part, block(order, i, k, half))
        idx = block(order, i, k)
        if r1 - r0 >= 32:
            rr = (r0, r0 + 32) if half == 0 else (r0 + 32, r1)
            return g.at[idx[0], idx[1], idx[2], core, rr[0]:rr[1], c0:c1]
        cc = (c0, c0 + 128) if half == 0 else (c0 + 128, c1)
        return g.at[idx[0], idx[1], idx[2], core, r0:r1, cc[0]:cc[1]]

    def to_sib(part, idx):
        v = view(part, idx)
        return go(v, v, sib)

    late = []
    for i in range(3):
        first = []
        for part in AG_PARTS:
            order = part[2]
            a = order[i]
            p = at[a]
            v = view(part, block(order, i, p))
            up = go(v, v, device(moved(at, a, 1), core))
            down = go(v, v, device(moved(at, a, -1), core))
            first.append((up, down))
        if i == 2:
            for part in AG_PARTS:
                late.append(to_sib(part, block(part[2], 2, at[part[2][2]])))
        second = []
        for part, (up, down) in zip(AG_PARTS, first):
            order = part[2]
            a = order[i]
            below, above = (at[a] + 3) % SIDE, (at[a] + 1) % SIDE
            up.wait_recv()
            v = half_view(part, i, below, 0)
            u2 = go(v, v, device(moved(at, a, 1), core))
            if i == 2:
                late.append(to_sib(part, block(order, 2, below)))
            down.wait_recv()
            v = half_view(part, i, above, 1)
            d2 = go(v, v, device(moved(at, a, -1), core))
            if i == 2:
                late.append(to_sib(part, block(order, 2, above)))
            second.append((u2, d2))
        for part, (u2, d2) in zip(AG_PARTS, second):
            order = part[2]
            u2.wait_recv()
            d2.wait_recv()
            if i == 2:
                late.append(to_sib(part, block(order, 2, (at[order[2]] + 2) % SIDE)))
    for c in late:
        c.wait_recv()
    for b in range(32):
        n = loc_ref[prompt * 32 + b]
        out_ref[b * 64:(b + 1) * 64, :] = g[n // 32, n // 8 % 4, n // 2 % 4, n % 2]


RS_PARTS = [((0, 48), (0, 1, 2)), ((48, 96), (1, 2, 0)), ((96, 128), (2, 0, 1))]


def scatter(go, held_ref, prompt_ref, x_ref, out_ref, w, peer, bufs):
    at, core = place()
    sib = device(at, 1 - core)
    swap = go(x_ref, peer, sib)
    mine, other = prompt_ref[device(at, core)], prompt_ref[sib]
    zero = jnp.zeros((128, 128), bf16)

    def fill(j, _):
        b = held_ref[j * 2 + core]
        w[j // 16, j // 4 % 4, j % 4] = jnp.where(b // 32 == mine, x_ref[b % 32], zero)
        return 0

    def more(j, _):
        b = held_ref[j * 2 + core]
        w[j // 16, j // 4 % 4, j % 4] += jnp.where(b // 32 == other, peer[b % 32], zero)
        return 0

    lax.fori_loop(0, 64, fill, 0)
    swap.wait_recv()
    lax.fori_loop(0, 64, more, 0)

    def spot(part, i, k, half=None):
        (r0, r1), order = part
        idx, free = [], None
        for a in range(3):
            if a in order[:i]:
                idx.append(at[a])
            elif a == order[i]:
                idx.append(k)
            else:
                free = a if free is None else free
                idx.append(slice(2 * half, 2 * half + 2) if half is not None and free == a else slice(0, SIDE))
        if half is not None and free is None:
            mid = r0 + (32 if r1 - r0 == 48 else 16)
            r0, r1 = (r0, mid) if half == 0 else (mid, r1)
        return (*idx, slice(r0, r1), slice(None))

    def inner(part, i, half):
        (r0, r1), _ = part
        if i < 2:
            return (slice(2 * half, 2 * half + 2),)
        mid = 32 if r1 - r0 == 48 else 16
        return (slice(0, mid) if half == 0 else slice(mid, r1 - r0),)

    for i in range(3):
        first = []
        for n, part in enumerate(RS_PARTS):
            a = part[1][i]
            p = at[a]
            up, down = device(moved(at, a, 1), core), device(moved(at, a, -1), core)
            far, above, below = (p + 2) % SIDE, (p + 1) % SIDE, (p + 3) % SIDE
            near_buf, far_buf = bufs[2 * (3 * n + i)], bufs[2 * (3 * n + i) + 1]
            f0 = go(w.at[spot(part, i, far, 0)], far_buf.at[(0, *inner(part, i, 0))], up)
            f1 = go(w.at[spot(part, i, far, 1)], far_buf.at[(1, *inner(part, i, 1))], down)
            n0 = go(w.at[spot(part, i, above, 1)], near_buf.at[(0, *inner(part, i, 1))], up)
            n1 = go(w.at[spot(part, i, below, 0)], near_buf.at[(1, *inner(part, i, 0))], down)
            first.append((f0, f1, n0, n1))
        second = []
        for n, (part, (f0, f1, n0, n1)) in enumerate(zip(RS_PARTS, first)):
            a = part[1][i]
            p = at[a]
            up, down = device(moved(at, a, 1), core), device(moved(at, a, -1), core)
            above, below = (p + 1) % SIDE, (p + 3) % SIDE
            near_buf, far_buf = bufs[2 * (3 * n + i)], bufs[2 * (3 * n + i) + 1]
            f0.wait_recv()
            w[spot(part, i, above, 0)] += far_buf[(0, *inner(part, i, 0))]
            s0 = go(w.at[spot(part, i, above, 0)], near_buf.at[(0, *inner(part, i, 0))], up)
            f1.wait_recv()
            w[spot(part, i, below, 1)] += far_buf[(1, *inner(part, i, 1))]
            s1 = go(w.at[spot(part, i, below, 1)], near_buf.at[(1, *inner(part, i, 1))], down)
            second.append((s0, s1))
        for n, (part, (f0, f1, n0, n1), (s0, s1)) in enumerate(zip(RS_PARTS, first, second)):
            for c in (n0, n1, s0, s1):
                c.wait_recv()
            near_buf = bufs[2 * (3 * n + i)]
            p = at[part[1][i]]
            total = (w[spot(part, i, p)].astype(f32) + near_buf[0].astype(f32)) + near_buf[1].astype(f32)
            if i < 2:
                w[spot(part, i, p)] = total.astype(bf16)
            else:
                (r0, r1), _ = part
                for s0, s1, col in ((r0, min(r1, 64), 0), (max(r0, 64), r1, 128)):
                    if s1 > s0:
                        out_ref[s0 % 64:s0 % 64 + s1 - s0, col:col + 128] = total[s0 - r0:s1 - r0]


def kernel(loc_ref, held_ref, prompt_ref, len_ref, q_ref, g_ref, rkv_ref, x_ref, o_ref, dq_ref, drkv_ref, out_ref,
           blocks, pkv, dpkv, kk, vv, kt, vt, s_scr, e_scr, dk, dv, w, peer, *rest):
    bufs, (send, recv) = rest[:-2], rest[-2:]
    at, core = place()
    me = device(at, core)
    enter(at, core)
    go = Sender(send, recv)
    gather(go, loc_ref, prompt_ref[me], x_ref, pkv, blocks)
    attend(len_ref[me], q_ref, g_ref, rkv_ref, pkv, o_ref, dq_ref, drkv_ref, dpkv, kk, vv, kt, vt, s_scr, e_scr, dk, dv)
    scatter(go, held_ref, prompt_ref, dpkv, out_ref, w, peer, bufs)
    go.drain()


def on_device(queries, resp_kv, prefix_kv, grad_out, held_block, resp_prompt, resp_len):
    spots = jnp.arange(128, dtype=jnp.int32)
    loc = jnp.sum(jnp.where(held_block[None, :] == spots[:, None], spots[None, :], 0), axis=1).astype(jnp.int32)
    rows, nk = queries.shape[0], 2048 + queries.shape[0]
    bufs = []
    for (r0, r1), order in RS_PARTS:
        for i in range(3):
            shape = (SIDE,) * (2 - i) + (r1 - r0, 128)
            bufs += [pltpu.VMEM((2,) + shape, bf16)] * 2
    sm = pl.BlockSpec(memory_space=pltpu.SMEM)
    vm = pl.BlockSpec(memory_space=pltpu.VMEM)
    return pl.pallas_call(
        kernel,
        out_shape=(jax.ShapeDtypeStruct(queries.shape, bf16), jax.ShapeDtypeStruct(queries.shape, bf16),
                   jax.ShapeDtypeStruct(resp_kv.shape, bf16), jax.ShapeDtypeStruct((64, 256), f32)),
        in_specs=[sm] * 4 + [vm] * 4,
        out_specs=(vm,) * 4,
        scratch_shapes=[pltpu.VMEM((4, 4, 4, 2, 64, 256), bf16), pltpu.VMEM((2048, 256), bf16),
                        pltpu.VMEM((32, 128, 128), bf16),
                        pltpu.VMEM((nk, 256), bf16), pltpu.VMEM((nk, 256), bf16), pltpu.VMEM((128, nk), bf16),
                        pltpu.VMEM((128, nk), bf16), pltpu.VMEM((nk, rows), f32), pltpu.VMEM((nk, rows), bf16),
                        pltpu.VMEM((nk, 128), f32), pltpu.VMEM((nk, 128), f32),
                        pltpu.VMEM((4, 4, 4, 128, 128), bf16), pltpu.VMEM((32, 128, 128), bf16)] + bufs
        + [pltpu.SemaphoreType.DMA((103,)), pltpu.SemaphoreType.DMA((103,))],
        compiler_params=pltpu.CompilerParams(collective_id=0, has_side_effects=True, vmem_limit_bytes=60 * 2**20),
        name="shared",
    )(loc, held_block, resp_prompt, resp_len, queries, grad_out, resp_kv, prefix_kv)


def solution(mesh):
    rows = P("dp", None)
    return jax.shard_map(on_device, mesh=mesh, in_specs=(rows, rows, rows, rows, P(), P(), P()),
                         out_specs=(rows, rows, rows, rows), check_vma=False)
```

time: 946 us -> 112 us (0.12)
  waiting for transfers between devices: 655 us -> 0 us
  local copies, waits for them, and re-layouts: 137 us -> 4.94 us
  matrix products: 104 us -> 0 us
  Pallas kernels: 0 us -> 104 us
  other arithmetic: 34.9 us -> 1.28 us
  between operations: 14.2 us -> 0.65 us
    reduce_scatter x1 -> x0, waiting for transfers between devices: 643 us -> none  [on_device(): lax.psum_scatter(jnp.where(matches[:, None], pref_grad[source], jnp.float...]
    pallas_call x0 -> x1, Pallas kernels: none -> 104 us  [on_device(): pl.pallas_call(kernel, out_shape=(jax.ShapeDtypeStruct(queries.shape, bf1...]
    dot_general x48 -> x0, matrix products: 104 us -> none  [the longest x8 22.8 us: one_block(): jnp.dot(query_block, key_rows.T, preferred_element_type=jnp.float32)]
    gather x2 -> x0, local copies, waits for them, and re-layouts: 80.4 us -> none  [the longest x1 48.9 us: on_device(): block = held_block[spots // block_rows]]
    scatter x1 -> x0, local copies, waits for them, and re-layouts: 36.2 us -> none  [on_device(): prefix = blank.at[where_to].set(piece, mode='drop')]
    select_n x5 -> x0, other arithmetic: 11.5 us -> none  [the longest x1 7.42 us: on_device(): jnp.where(matches[:, None], pref_grad[source], jnp.float32(0.0))]
    all_gather x1 -> x0, waiting for transfers between devices: 11.1 us -> none  [on_device(): piece = lax.all_gather(prefix_kv, 'dp', axis=0, tiled=True)]
    div x8 -> x0, other arithmetic: 9.67 us -> none  [one_block(): weights = exponent / jnp.sum(exponent, axis=1, keepdims=True)]
  transfers between devices with their start and end apart: 2 -> 0, of which waited for: 2 -> 0; matrix products, arithmetic and copies ran while one was open for 7% -> 0% of each run, Pallas kernels for 0% -> 0%
where the time goes in v1:
time: 112 us; the launch traced here: 111 us
  Pallas kernels  104 us (93%)
  local copies, waits for them, and re-layouts  4.94 us (4%)
  other arithmetic  1.28 us (1%)
    pallas_call x1, Pallas kernels, on_device(): pl.pallas_call(kernel, out_shape=(jax.ShapeDtypeStruct(queries.shape, bf1...  104 us
    unnamed x10, local copies, waits for them, and re-layouts  4.94 us

profile of v1, /device:TPU:0, one launch (start us, length us, event | category | flops | bytes accessed | tf_op | source)
XLA Modules:
  0.0 111.3 jit_solution(8174108014932244817)
XLA Ops:
  0.6 1.3 %select_reduce_fusion.loc_ref = s32[128]{0:T(128)} fusion(s32[128]{0:T(128)} %held_ref.1), kind=kLoop, calls=%fused_computation | loop fusion | flops 49024 | bytes 1024 | tf_op jit(solution)/shard_map/reduce_sum | solution.py:349
  1.9 104.4 %shared.1 = (bf16[512,1024]{1,0:T(8,128)(2,1)}, bf16[512,1024]{1,0:T(8,128)(2,1)}, bf16[512,256]{1,0:T(8,128)(2,1)}, f32[64,256]{1,0:T(8,128)}) custom-call(s32[128]{0:T(128)} %select_reduce_fusion.loc_ref, s32[128]{0:T(128)} %held_ref.1, s32[128]{0:T(128)} %prompt_ref.1, s32[128]{0:T(128)} %len_ref.1, bf16[512,1024]{1,0:T(8,128)(2,1)} %q_ref.1, ...), custom_call_target="tpu_custom_call" | custom-call | tf_op jit(solution)/shard_map/shared/pallas_call | solution.py:358
  106.3 0.0 copy-start
  106.3 2.4 %copy.15 = bf16[512,1024]{1,0:T(8,128)(2,1)} copy(bf16[512,1024]{1,0:T(8,128)(2,1)} %get-tuple-element.8) | data formatting | bytes 2097152
  108.7 0.0 copy-done
  108.7 0.0 copy-start.1
  108.7 1.0 copy.16
  109.6 0.1 copy-done.1
  109.8 0.0 copy-start.2
  109.8 0.7 copy.17
  110.5 0.2 copy-done.2
  110.6 0.6 copy.18
Async XLA Ops:
  106.3 2.4 %copy-start = (bf16[512,1024]{1,0:T(8,128)(2,1)S(1)}, bf16[512,1024]{1,0:T(8,128)(2,1)}, u32[]{:S(2)}) copy-start(bf16[512,1024]{1,0:T(8,128)(2,1)} %get-tuple-element.9) | copy-start | bytes 3145732
  108.7 1.1 copy-start.1
  109.8 0.9 copy-start.2

commit v2 on v0

v2 whole, which is shorter than its diff:
```python
import math

import jax
import jax.numpy as jnp
from jax import lax
from jax.experimental import pallas as pl
from jax.experimental.pallas import tpu as pltpu
from jax.sharding import PartitionSpec as P

f32, bf16 = jnp.float32, jnp.bfloat16
MESH = pl.DeviceIdType.MESH
NN = (((1,), (0,)), ((), ()))
SIDE = 4
D = 128
HEADS = 8
ROWS = 512
BLOCKS = 32
CHUNKS = 4
CK = 512
PK = CHUNKS * CK
NK = PK + ROWS
HALF = ROWS // 2
UNROLL = 4
SCALE = 1.0 / math.sqrt(D)
LOG2 = SCALE * math.log2(math.e)
ORDERS = ((0, 1, 2), (1, 2, 0), (2, 0, 1))
HOPS = (2, 1, 3)
PARTS = [(c, t) for c in range(CHUNKS) for t in range(2)]


def mm(a, b):
    return lax.dot_general(a, b, NN, preferred_element_type=f32)


def place():
    me = lax.axis_index("dp")
    return (me // 32, me // 8 % SIDE, me // 2 % SIDE), me % 2


def device(at, core):
    return ((at[0] * SIDE + at[1]) * SIDE + at[2]) * 2 + core


def moved(at, axis, step):
    return tuple((c + step) % SIDE if a == axis else c for a, c in enumerate(at))


class Sender:
    def __init__(self, send, recv):
        self.send, self.recv, self.count, self.all = send, recv, 0, []

    def __call__(self, src, dst, to):
        i = self.count
        self.count += 1
        c = pltpu.make_async_remote_copy(src_ref=src, dst_ref=dst, send_sem=self.send.at[i], recv_sem=self.recv.at[i],
                                         device_id=(to,), device_id_type=MESH)
        c.start()
        self.all.append(c)
        return c

    def drain(self):
        for c in self.all:
            c.wait_send()


class Gather:
    def __init__(self, go, at, core, refs):
        self.go, self.at, self.core, self.refs = go, at, core, refs
        self.flying = {}

    def order(self, n):
        return ORDERS[(n + 1) % 3]

    def view(self, n, i, k):
        order = self.order(n)
        idx = [slice(0, SIDE) if a in order[:i] else k if a == order[i] else self.at[a] for a in range(3)]
        return self.refs[n].at[(self.core, *idx)]

    def start(self, n, i):
        a = self.order(n)[i]
        v = self.view(n, i, self.at[a])
        self.flying[n, i] = [self.go(v, v, device(moved(self.at, a, s), self.core)) for s in HOPS]

    def wait(self, n, i):
        for c in self.flying[n, i]:
            c.wait_recv()

    def start_core(self, n):
        v = self.refs[n].at[self.core]
        self.flying[n, 3] = [self.go(v, v, device(self.at, 1 - self.core))]


class Scatter:
    def __init__(self, go, at, core, held, prompt, own, peer, w, bufs, out):
        self.go, self.at, self.core, self.held, self.prompt = go, at, core, held, prompt
        self.own, self.peer, self.w, self.bufs, self.out = own, peer, w, bufs, out
        self.flying = {}

    def swap(self, c):
        self.flying[c] = self.go(self.own[c], self.peer[c], device(self.at, 1 - self.core))

    def fill(self, c):
        self.flying[c].wait_recv()
        mine = self.prompt[device(self.at, self.core)]
        other = self.prompt[device(self.at, 1 - self.core)]
        own, peer, w = self.own[c], self.peer[c], self.w[c]
        zero = jnp.zeros((32, D), bf16)

        def body(j, _):
            for u in range(4):
                b = self.held[(j * 4 + u) * 2 + self.core]
                p, k = lax.shift_right_logical(b, 5), lax.bitwise_and(b, 31)
                w[j // 4, j % 4, u] = jnp.where(p == mine, own[k], zero) + jnp.where(p == other, peer[k], zero)
            return 0

        lax.fori_loop(0, 16, body, 0)

    def spot(self, n, i, k):
        c, t = PARTS[n]
        order = ORDERS[n % 3]
        idx = [self.at[a] if a in order[:i] else k if a == order[i] else slice(0, SIDE) for a in range(3)]
        return (*idx, slice(16 * t, 16 * t + 16), slice(None))

    def start(self, c, i):
        for n in (2 * c, 2 * c + 1):
            a = ORDERS[n % 3][i]
            self.flying[n, i] = [
                self.go(self.w[c].at[self.spot(n, i, (self.at[a] + s) % SIDE)], self.bufs[3 * n + i].at[j],
                        device(moved(self.at, a, s), self.core)) for j, s in enumerate(HOPS)]

    def add(self, c, i):
        for n in (2 * c, 2 * c + 1):
            for f in self.flying[n, i]:
                f.wait_recv()
            buf = self.bufs[3 * n + i]
            here = self.spot(n, i, self.at[ORDERS[n % 3][i]])
            total = (self.w[c][here].astype(f32) + buf[0].astype(f32)) + (buf[1].astype(f32) + buf[2].astype(f32))
            if i < 2:
                self.w[c][here] = total.astype(bf16)
            else:
                t = n % 2
                self.out[16 * c:16 * c + 16, D * t:D * t + D] = total

    def stage(self, c, s):
        if s == 0:
            self.fill(c)
            self.start(c, 0)
        else:
            self.add(c, s - 1)
            if s < 3:
                self.start(c, s)


def kernel(loc_ref, held_ref, prompt_ref, len_ref, q_hbm, g_hbm, rkv_ref, x_ref, o_ref, dq_ref, drkv_ref, out_ref, *rest):
    gref, rest = rest[:8], rest[8:]
    own, peer, w, bufs, rest = rest[:4], rest[4:8], rest[8:12], rest[12:36], rest[36:]
    q_ref, g_ref, kk, vv, kt, vt, q2t, g2t, gp, e_all, ms, ls, ot, dqt, dk, dv, s0, s1, p0, p1, send, recv, local = rest
    at, core = place()
    me = device(at, core)
    barrier = pltpu.get_barrier_semaphore()
    near = [device(moved(at, a, s), core) for a in range(3) for s in HOPS] + [device(at, 1 - core)]
    for n in near:
        pl.semaphore_signal(barrier, inc=1, device_id=(n,), device_id_type=MESH)
    q_in = pltpu.make_async_copy(q_hbm, q_ref, local.at[0])
    g_in = pltpu.make_async_copy(g_hbm, g_ref, local.at[1])
    q_in.start()
    g_in.start()
    go = Sender(send, recv)
    gather = Gather(go, at, core, gref)
    for n, (c, t) in enumerate(PARTS):
        gref[n][core, at[0], at[1], at[2]] = x_ref[16 * c:16 * c + 16, D * t:D * t + D]
    pl.semaphore_wait(barrier, len(near))
    for n in range(8):
        gather.start(n, 0)

    length = len_ref[me]
    live = lax.broadcasted_iota(jnp.int32, (1, ROWS), 1) < length
    tri = lax.broadcasted_iota(jnp.int32, (HALF, HALF), 0) <= lax.broadcasted_iota(jnp.int32, (HALF, HALF), 1)
    vv[:, D:] = jnp.ones((NK, D), bf16)

    def heads_loop(lo, hi, item, step=UNROLL):
        def body(i, _):
            for u in range(step):
                item(i * step + u)
            return 0
        lax.fori_loop(lo // step, hi // step, body, 0)

    def staged(ahead, item, slots):
        slots[0][...] = ahead(0)

        def body(i, _):
            for u in range(UNROLL):
                h = i * UNROLL + u
                slots[(u + 1) % 2][...] = ahead(lax.rem(h + 1, HEADS))
                item(h, slots[u % 2])
            return 0
        lax.fori_loop(0, HEADS // UNROLL, body, 0)

    def cols(h):
        return pl.ds(pl.multiple_of(h * D, D), D)

    def prepare(h):
        qs = q_ref[:, cols(h)].astype(f32) * LOG2
        hi = qs.astype(bf16)
        lo = (qs - hi.astype(f32)).astype(bf16)
        q2t[h, 0:D] = hi.T
        q2t[h, D:] = lo.T

    def place_keys(k0, kn, keys, vals):
        kk[k0:k0 + kn, 0:D] = keys
        kk[k0:k0 + kn, D:] = keys
        vv[k0:k0 + kn, 0:D] = vals

    def turn(k0, kn):
        kt[:, k0:k0 + kn] = kk[k0:k0 + kn, 0:D].T
        vt[:, k0:k0 + kn] = vv[k0:k0 + kn, 0:D].T

    def first(h):
        sa = mm(kk[PK:PK + HALF, :], q2t[h])
        sa = jnp.concatenate([jnp.where(tri, sa[:, :HALF], -1e30), sa[:, HALF:]], axis=1)
        sb = jnp.where(tri, mm(kk[PK + HALF:, :], q2t[h, :, HALF:]), -1e30)
        m = jnp.max(sa, axis=0, keepdims=True)
        m = jnp.concatenate([m[:, :HALF], jnp.maximum(m[:, HALF:], jnp.max(sb, axis=0, keepdims=True))], axis=1)
        ea = jnp.exp2(sa - m)
        eb = jnp.exp2(sb - m[:, HALF:])
        l = jnp.sum(ea, axis=0, keepdims=True)
        l = jnp.concatenate([l[:, :HALF], l[:, HALF:] + jnp.sum(eb, axis=0, keepdims=True)], axis=1)
        ea, eb = ea.astype(bf16), eb.astype(bf16)
        e_all[h, PK:PK + HALF, :] = ea
        e_all[h, PK + HALF:, HALF:] = eb
        oa = mm(vt[:, PK:PK + HALF], ea)
        ob = mm(vt[:, PK + HALF:], eb)
        ms[0, h] = m
        ls[h] = l
        ot[h, :, 0:HALF] = oa[:, :HALF]
        ot[h, :, HALF:] = oa[:, HALF:] + ob

    def forward(c):
        k0 = c * CK

        def ahead(h):
            return mm(kk[k0:k0 + CK, :], q2t[h])

        def item(h, s):
            old = ms[c, h]
            m = jnp.maximum(old, jnp.max(s[...], axis=0, keepdims=True))
            e = jnp.exp2(s[...] - m)
            fade = jnp.exp2(old - m)
            ls[h] = ls[h] * fade + jnp.sum(e, axis=0, keepdims=True)
            e = e.astype(bf16)
            e_all[h, k0:k0 + CK, :] = e
            ot[h] = ot[h] * fade + mm(vt[:, k0:k0 + CK], e)
            ms[c + 1, h] = m
        staged(ahead, item, (s0, s1))

    def finish(h):
        f = jnp.where(live, 1.0 / ls[h], 0.0)
        o = ot[h] * f
        o_ref[:, cols(h)] = o.astype(bf16).T
        gt = g_ref[:, cols(h)].T.astype(f32)
        gt = jnp.where(live, gt, 0.0) * f
        neg = -jnp.sum(gt * o, axis=0, keepdims=True)
        gb = gt.astype(bf16)
        gp[h] = gb.T
        hi = neg.astype(bf16).astype(f32)
        sub = lax.broadcasted_iota(jnp.int32, (16, ROWS), 0)
        extra = jnp.where(sub == 0, hi, jnp.where(sub == 1, neg - hi, 0.0)).astype(bf16)
        g2t[h, 0:D] = gb
        g2t[h, D:D + 16] = extra
        g2t[h, D + 16:] = jnp.zeros((D - 16, ROWS), bf16)
        dqt[h] = jnp.zeros((D, ROWS), f32)

    def slope(h, k0, kn, r0):
        return mm(vv[k0:k0 + kn, :], g2t[h, :, r0:]).astype(bf16)

    def back(h, dp, k0, kn, r0, stage, a0):
        fade = jnp.exp2(ms[stage, h] - ms[CHUNKS, h]).astype(bf16)[:, r0:]
        e = e_all[h, k0:k0 + kn, r0:] * fade
        ds = e * dp
        dqt[h, :, r0:] += mm(kt[:, k0:k0 + kn], ds)
        dk[a0:a0 + kn, :] += mm(ds, q_ref[r0:, cols(h)])
        dv[a0:a0 + kn, :] += mm(e, gp[h, r0:, :])

    def load_chunk(c):
        for n in (2 * c, 2 * c + 1):
            gather.wait(n, 3)
        prompt = prompt_ref[me]
        for b in range(BLOCKS):
            n = loc_ref[prompt * BLOCKS + b]
            idx = (lax.bitwise_and(n, 1), lax.shift_right_logical(n, 5), lax.bitwise_and(lax.shift_right_logical(n, 3), 3),
                   lax.bitwise_and(lax.shift_right_logical(n, 1), 3))
            place_keys(c * CK + 16 * b, 16, gref[2 * c][idx], gref[2 * c + 1][idx])
        turn(c * CK, CK)

    place_keys(PK, ROWS, rkv_ref[:, 0:D], rkv_ref[:, D:])
    turn(PK, ROWS)
    q_in.wait()
    heads_loop(0, HEADS, prepare)
    for n in range(8):
        gather.wait(n, 0)
        gather.start(n, 1)
    heads_loop(0, 4, first)
    for n in range(8):
        gather.wait(n, 1)
        gather.start(n, 2)
    heads_loop(4, HEADS, first)

    def pass_on(c):
        for n in (2 * c, 2 * c + 1):
            gather.wait(n, 2)
            gather.start_core(n)

    pass_on(0)
    for c in range(CHUNKS):
        load_chunk(c)
        if c + 1 < CHUNKS:
            pass_on(c + 1)
        forward(c)
    g_in.wait()
    heads_loop(0, HEADS, finish)

    scatter = Scatter(go, at, core, held_ref, prompt_ref, own, peer, w, bufs, out_ref)
    for c in range(CHUNKS):
        dk[...] = jnp.zeros_like(dk)
        dv[...] = jnp.zeros_like(dv)
        staged(lambda h: slope(h, c * CK, CK, 0), lambda h, dp: back(h, dp[...], c * CK, CK, 0, c + 1, 0), (p0, p1))
        own[c][:, 0:16, :] = (dk[...] * SCALE).astype(bf16).reshape(BLOCKS, 16, D)
        own[c][:, 16:, :] = dv[...].astype(bf16).reshape(BLOCKS, 16, D)
        scatter.swap(c)
        for s in range(c):
            scatter.stage(c - 1 - s, s)
    dk[...] = jnp.zeros_like(dk)
    dv[...] = jnp.zeros_like(dv)

    def last(h):
        back(h, slope(h, PK, HALF, 0), PK, HALF, 0, 0, 0)
        back(h, slope(h, PK + HALF, HALF, HALF), PK + HALF, HALF, HALF, 0, HALF)
        dq_ref[:, cols(h)] = (dqt[h] * SCALE).astype(bf16).T

    heads_loop(0, 4, last)
    for s in range(4):
        scatter.stage(3 - s, s)
    heads_loop(4, HEADS, last)
    for s in range(1, 4):
        scatter.stage(4 - s, s)
    drkv_ref[:, 0:D] = (dk[...] * SCALE).astype(bf16)
    drkv_ref[:, D:] = dv[...].astype(bf16)
    scatter.stage(3, 2)
    scatter.stage(2, 3)
    scatter.stage(3, 3)
    go.drain()


def on_device(queries, resp_kv, prefix_kv, grad_out, held_block, resp_prompt, resp_len):
    spots = jnp.arange(128, dtype=jnp.int32)
    loc = jnp.sum(jnp.where(held_block[None, :] == spots[:, None], spots[None, :], 0), axis=1).astype(jnp.int32)
    bufs = []
    for n in range(8):
        for i in range(3):
            bufs.append(pltpu.VMEM((3,) + (SIDE,) * (2 - i) + (16, D), bf16))
    sm = pl.BlockSpec(memory_space=pltpu.SMEM)
    vm = pl.BlockSpec(memory_space=pltpu.VMEM)
    hbm = pl.BlockSpec(memory_space=pl.ANY)
    sems = 8 * 10 + 8 * 9 + 4
    return pl.pallas_call(
        kernel,
        out_shape=(jax.ShapeDtypeStruct(queries.shape, bf16), jax.ShapeDtypeStruct(queries.shape, bf16),
                   jax.ShapeDtypeStruct(resp_kv.shape, bf16), jax.ShapeDtypeStruct((64, 256), f32)),
        in_specs=[sm] * 4 + [hbm] * 2 + [vm] * 2,
        out_specs=(vm,) * 4,
        scratch_shapes=[pltpu.VMEM((2, SIDE, SIDE, SIDE, 16, D), bf16)] * 8
        + [pltpu.VMEM((BLOCKS, 32, D), bf16)] * 8 + [pltpu.VMEM((SIDE, SIDE, SIDE, 32, D), bf16)] * 4 + bufs
        + [pltpu.VMEM((ROWS, HEADS * D), bf16), pltpu.VMEM((ROWS, HEADS * D), bf16),
           pltpu.VMEM((NK, 2 * D), bf16), pltpu.VMEM((NK, 2 * D), bf16), pltpu.VMEM((D, NK), bf16),
           pltpu.VMEM((D, NK), bf16), pltpu.VMEM((HEADS, 2 * D, ROWS), bf16), pltpu.VMEM((HEADS, 2 * D, ROWS), bf16),
           pltpu.VMEM((HEADS, ROWS, D), bf16), pltpu.VMEM((HEADS, NK, ROWS), bf16),
           pltpu.VMEM((CHUNKS + 1, HEADS, 1, ROWS), f32), pltpu.VMEM((HEADS, 1, ROWS), f32),
           pltpu.VMEM((HEADS, D, ROWS), f32), pltpu.VMEM((HEADS, D, ROWS), f32),
           pltpu.VMEM((ROWS, D), f32), pltpu.VMEM((ROWS, D), f32),
           pltpu.VMEM((CK, ROWS), f32), pltpu.VMEM((CK, ROWS), f32), pltpu.VMEM((CK, ROWS), bf16), pltpu.VMEM((CK, ROWS), bf16),
           pltpu.SemaphoreType.DMA((sems,)), pltpu.SemaphoreType.DMA((sems,)), pltpu.SemaphoreType.DMA((2,))],
        compiler_params=pltpu.CompilerParams(collective_id=0, has_side_effects=True, vmem_limit_bytes=62 * 2**20),
        name="shared",
    )(loc, held_block, resp_prompt, resp_len, queries, grad_out, resp_kv, prefix_kv)


def solution(mesh):
    rows = P("dp", None)
    return jax.shard_map(on_device, mesh=mesh, in_specs=(rows, rows, rows, rows, P(), P(), P()),
                         out_specs=(rows, rows, rows, rows), check_vma=False)
```

time: 946 us -> 85.1 us (0.09)
  waiting for transfers between devices: 655 us -> 0 us
  local copies, waits for them, and re-layouts: 137 us -> 4.94 us
  matrix products: 104 us -> 0 us
  Pallas kernels: 0 us -> 78 us
  other arithmetic: 34.9 us -> 1.28 us
  between operations: 14.2 us -> 0.65 us
    reduce_scatter x1 -> x0, waiting for transfers between devices: 643 us -> none  [on_device(): lax.psum_scatter(jnp.where(matches[:, None], pref_grad[source], jnp.float...]
    dot_general x48 -> x0, matrix products: 104 us -> none  [the longest x8 22.8 us: one_block(): jnp.dot(query_block, key_rows.T, preferred_element_type=jnp.float32)]
    gather x2 -> x0, local copies, waits for them, and re-layouts: 80.4 us -> none  [the longest x1 48.9 us: on_device(): block = held_block[spots // block_rows]]
    pallas_call x0 -> x1, Pallas kernels: none -> 78 us  [on_device(): pl.pallas_call(kernel, out_shape=(jax.ShapeDtypeStruct(queries.shape, bf1...]
    scatter x1 -> x0, local copies, waits for them, and re-layouts: 36.2 us -> none  [on_device(): prefix = blank.at[where_to].set(piece, mode='drop')]
    select_n x5 -> x0, other arithmetic: 11.5 us -> none  [the longest x1 7.42 us: on_device(): jnp.where(matches[:, None], pref_grad[source], jnp.float32(0.0))]
    all_gather x1 -> x0, waiting for transfers between devices: 11.1 us -> none  [on_device(): piece = lax.all_gather(prefix_kv, 'dp', axis=0, tiled=True)]
    div x8 -> x0, other arithmetic: 9.67 us -> none  [one_block(): weights = exponent / jnp.sum(exponent, axis=1, keepdims=True)]
  transfers between devices with their start and end apart: 2 -> 0, of which waited for: 2 -> 0; matrix products, arithmetic and copies ran while one was open for 7% -> 0% of each run, Pallas kernels for 0% -> 0%
where the time goes in v2:
time: 85.1 us; the launch traced here: 84.8 us
  Pallas kernels  78 us (92%)
  local copies, waits for them, and re-layouts  4.94 us (6%)
  other arithmetic  1.28 us (2%)
    pallas_call x1, Pallas kernels, on_device(): pl.pallas_call(kernel, out_shape=(jax.ShapeDtypeStruct(queries.shape, bf1...  78 us
    unnamed x10, local copies, waits for them, and re-layouts  4.94 us

profile of v2, /device:TPU:0, one launch (start us, length us, event | category | flops | bytes accessed | tf_op | source)
XLA Modules:
  0.0 84.8 jit_solution(3587071170299105691)
XLA Ops:
  0.6 1.3 %select_reduce_fusion.loc_ref = s32[128]{0:T(128)} fusion(s32[128]{0:T(128)} %held_ref.1), kind=kLoop, calls=%fused_computation | loop fusion | flops 49024 | bytes 1024 | tf_op jit(solution)/shard_map/reduce_sum | solution.py:356
  1.9 78.0 %shared.1 = (bf16[512,1024]{1,0:T(8,128)(2,1)}, bf16[512,1024]{1,0:T(8,128)(2,1)}, bf16[512,256]{1,0:T(8,128)(2,1)}, f32[64,256]{1,0:T(8,128)}) custom-call(s32[128]{0:T(128)} %select_reduce_fusion.loc_ref, s32[128]{0:T(128)} %held_ref.1, s32[128]{0:T(128)} %prompt_ref.1, s32[128]{0:T(128)} %len_ref.1, bf16[512,1024]{1,0:T(8,128)(2,1)} %q_hbm.1, ...), custom_call_target="tpu_custom_call" | custom-call | tf_op jit(solution)/shard_map/shared/pallas_call | solution.py:365
  79.9 0.0 copy-start
  79.9 2.4 %copy.15 = bf16[512,1024]{1,0:T(8,128)(2,1)} copy(bf16[512,1024]{1,0:T(8,128)(2,1)} %get-tuple-element.8) | data formatting | bytes 2097152
  82.2 0.0 copy-done
  82.2 0.0 copy-start.1
  82.2 1.0 %copy.16 = bf16[512,1024]{1,0:T(8,128)(2,1)} copy(bf16[512,1024]{1,0:T(8,128)(2,1)S(1)} %copy-done) | data formatting | bytes 2097152
  83.2 0.1 copy-done.1
  83.3 0.0 copy-start.2
  83.3 0.7 copy.17
  84.0 0.2 copy-done.2
  84.2 0.6 copy.18
Async XLA Ops:
  79.9 2.4 %copy-start = (bf16[512,1024]{1,0:T(8,128)(2,1)S(1)}, bf16[512,1024]{1,0:T(8,128)(2,1)}, u32[]{:S(2)}) copy-start(bf16[512,1024]{1,0:T(8,128)(2,1)} %get-tuple-element.9) | copy-start | bytes 3145732
  82.2 1.1 %copy-start.1 = (bf16[512,256]{1,0:T(8,128)(2,1)S(1)}, bf16[512,256]{1,0:T(8,128)(2,1)}, u32[]{:S(2)}) copy-start(bf16[512,256]{1,0:T(8,128)(2,1)} %get-tuple-element.10) | copy-start | bytes 786436
  83.3 0.9 %copy-start.2 = (f32[64,256]{1,0:T(8,128)S(1)}, f32[64,256]{1,0:T(8,128)}, u32[]{:S(2)}) copy-start(f32[64,256]{1,0:T(8,128)} %get-tuple-element.11) | copy-start | bytes 196612

commit v3 on v2

--- a/solution.py
+++ b/solution.py
@@ -50,11 +50,15 @@
         self.send, self.recv, self.count, self.all = send, recv, 0, []
 
     def __call__(self, src, dst, to):
+        c = self.ready(src, dst, to)
+        c.start()
+        return c
+
+    def ready(self, src, dst, to):
         i = self.count
         self.count += 1
         c = pltpu.make_async_remote_copy(src_ref=src, dst_ref=dst, send_sem=self.send.at[i], recv_sem=self.recv.at[i],
                                          device_id=(to,), device_id_type=MESH)
-        c.start()
         self.all.append(c)
         return c
 
@@ -64,30 +68,33 @@
 
 
 class Gather:
-    def __init__(self, go, at, core, refs):
-        self.go, self.at, self.core, self.refs = go, at, core, refs
+    def __init__(self, go, at, core, refs, stages):
+        self.go, self.at, self.core, self.refs, self.stages = go, at, core, refs, stages
         self.flying = {}
 
-    def order(self, n):
-        return ORDERS[(n + 1) % 3]
-
-    def view(self, n, i, k):
-        order = self.order(n)
-        idx = [slice(0, SIDE) if a in order[:i] else k if a == order[i] else self.at[a] for a in range(3)]
-        return self.refs[n].at[(self.core, *idx)]
-
-    def start(self, n, i):
-        a = self.order(n)[i]
-        v = self.view(n, i, self.at[a])
-        self.flying[n, i] = [self.go(v, v, device(moved(self.at, a, s), self.core)) for s in HOPS]
-
-    def wait(self, n, i):
-        for c in self.flying[n, i]:
+    def put(self, x_ref):
+        for n, (c, t) in enumerate(PARTS):
+            a, b, _ = ORDERS[n % 3]
+            self.stages[n % 3][self.at[a], self.at[b], n // 3] = x_ref[16 * c:16 * c + 16, D * t:D * t + D]
+
+    def start(self, k, i):
+        a, b, _ = ORDERS[k]
+        v = self.stages[k].at[self.at[a], self.at[b]] if i == 0 else self.stages[k].at[:, self.at[b]]
+        self.flying[k, i] = [self.go(v, v, device(moved(self.at, ORDERS[k][i], s), self.core)) for s in HOPS]
+
+    def start_last(self, n):
+        a = ORDERS[n % 3][2]
+        src, dst = self.stages[n % 3].at[:, :, n // 3], self.refs[n].at[self.core, self.at[a]]
+        self.flying["part", n] = [self.go(src, dst, device(moved(self.at, a, s), self.core)) for s in HOPS]
+        self.refs[n][self.core, self.at[a]] = self.stages[n % 3][:, :, n // 3]
+
+    def wait(self, *key):
+        for c in self.flying[key]:
             c.wait_recv()
 
     def start_core(self, n):
         v = self.refs[n].at[self.core]
-        self.flying[n, 3] = [self.go(v, v, device(self.at, 1 - self.core))]
+        self.flying["core", n] = [self.go(v, v, device(self.at, 1 - self.core))]
 
 
 class Scatter:
@@ -95,9 +102,12 @@
         self.go, self.at, self.core, self.held, self.prompt = go, at, core, held, prompt
         self.own, self.peer, self.w, self.bufs, self.out = own, peer, w, bufs, out
         self.flying = {}
+        self.coord = [[(at[a] + s) % SIDE for s in HOPS] for a in range(3)]
+        self.dev = [[device(moved(at, a, s), core) for s in HOPS] for a in range(3)]
+        self.other_core = device(at, 1 - core)
 
     def swap(self, c):
-        self.flying[c] = self.go(self.own[c], self.peer[c], device(self.at, 1 - self.core))
+        self.flying[c] = self.go(self.own[c], self.peer[c], self.other_core)
 
     def fill(self, c):
         self.flying[c].wait_recv()
@@ -121,12 +131,19 @@
         idx = [self.at[a] if a in order[:i] else k if a == order[i] else slice(0, SIDE) for a in range(3)]
         return (*idx, slice(16 * t, 16 * t + 16), slice(None))
 
-    def start(self, c, i):
+    def ready(self, c, i):
         for n in (2 * c, 2 * c + 1):
             a = ORDERS[n % 3][i]
             self.flying[n, i] = [
-                self.go(self.w[c].at[self.spot(n, i, (self.at[a] + s) % SIDE)], self.bufs[3 * n + i].at[j],
-                        device(moved(self.at, a, s), self.core)) for j, s in enumerate(HOPS)]
+                self.go.ready(self.w[c].at[self.spot(n, i, self.coord[a][j])], self.bufs[3 * n + i].at[j], self.dev[a][j])
+                for j in range(3)]
+
+    def start(self, c, i):
+        if (2 * c, i) not in self.flying:
+            self.ready(c, i)
+        for n in (2 * c, 2 * c + 1):
+            for f in self.flying[n, i]:
+                f.start()
 
     def add(self, c, i):
         for n in (2 * c, 2 * c + 1):
@@ -151,10 +168,10 @@
                 self.start(c, s)
 
 
-def kernel(loc_ref, held_ref, prompt_ref, len_ref, q_hbm, g_hbm, rkv_ref, x_ref, o_ref, dq_ref, drkv_ref, out_ref, *rest):
-    gref, rest = rest[:8], rest[8:]
+def kernel(loc_ref, held_ref, prompt_ref, len_ref, q_hbm, g_hbm, rkv_ref, x_ref, o_hbm, dq_hbm, drkv_hbm, out_ref, *rest):
+    gref, stages, rest = rest[:8], rest[8:11], rest[11:]
     own, peer, w, bufs, rest = rest[:4], rest[4:8], rest[8:12], rest[12:36], rest[36:]
-    q_ref, g_ref, kk, vv, kt, vt, q2t, g2t, gp, e_all, ms, ls, ot, dqt, dk, dv, s0, s1, p0, p1, send, recv, local = rest
+    q_ref, g_ref, kk, vv, kt, vt, q2t, g2t, gp, e_all, ms, ls, ot, o_ref, dq_ref, drkv_ref, dk, dv, s0, s1, p0, p1, send, recv, local = rest
     at, core = place()
     me = device(at, core)
     barrier = pltpu.get_barrier_semaphore()
@@ -166,12 +183,11 @@
     q_in.start()
     g_in.start()
     go = Sender(send, recv)
-    gather = Gather(go, at, core, gref)
-    for n, (c, t) in enumerate(PARTS):
-        gref[n][core, at[0], at[1], at[2]] = x_ref[16 * c:16 * c + 16, D * t:D * t + D]
+    gather = Gather(go, at, core, gref, stages)
+    gather.put(x_ref)
     pl.semaphore_wait(barrier, len(near))
-    for n in range(8):
-        gather.start(n, 0)
+    for k in range(3):
+        gather.start(k, 0)
 
     length = len_ref[me]
     live = lax.broadcasted_iota(jnp.int32, (1, ROWS), 1) < length
@@ -185,10 +201,12 @@
             return 0
         lax.fori_loop(lo // step, hi // step, body, 0)
 
-    def staged(ahead, item, slots):
+    def staged(ahead, item, slots, middle=None):
         slots[0][...] = ahead(0)
 
         def body(i, _):
+            if middle is not None:
+                pl.when(i == 1)(middle)
             for u in range(UNROLL):
                 h = i * UNROLL + u
                 slots[(u + 1) % 2][...] = ahead(lax.rem(h + 1, HEADS))
@@ -256,7 +274,7 @@
     def finish(h):
         f = jnp.where(live, 1.0 / ls[h], 0.0)
         o = ot[h] * f
-        o_ref[:, cols(h)] = o.astype(bf16).T
+        ot[h] = o
         gt = g_ref[:, cols(h)].T.astype(f32)
         gt = jnp.where(live, gt, 0.0) * f
         neg = -jnp.sum(gt * o, axis=0, keepdims=True)
@@ -268,7 +286,6 @@
         g2t[h, 0:D] = gb
         g2t[h, D:D + 16] = extra
         g2t[h, D + 16:] = jnp.zeros((D - 16, ROWS), bf16)
-        dqt[h] = jnp.zeros((D, ROWS), f32)
 
     def slope(h, k0, kn, r0):
         return mm(vv[k0:k0 + kn, :], g2t[h, :, r0:]).astype(bf16)
@@ -277,37 +294,40 @@
         fade = jnp.exp2(ms[stage, h] - ms[CHUNKS, h]).astype(bf16)[:, r0:]
         e = e_all[h, k0:k0 + kn, r0:] * fade
         ds = e * dp
-        dqt[h, :, r0:] += mm(kt[:, k0:k0 + kn], ds)
+        e_all[h, k0:k0 + kn, r0:] = ds
         dk[a0:a0 + kn, :] += mm(ds, q_ref[r0:, cols(h)])
         dv[a0:a0 + kn, :] += mm(e, gp[h, r0:, :])
 
     def load_chunk(c):
         for n in (2 * c, 2 * c + 1):
-            gather.wait(n, 3)
+            gather.wait("core", n)
         prompt = prompt_ref[me]
         for b in range(BLOCKS):
             n = loc_ref[prompt * BLOCKS + b]
-            idx = (lax.bitwise_and(n, 1), lax.shift_right_logical(n, 5), lax.bitwise_and(lax.shift_right_logical(n, 3), 3),
-                   lax.bitwise_and(lax.shift_right_logical(n, 1), 3))
-            place_keys(c * CK + 16 * b, 16, gref[2 * c][idx], gref[2 * c + 1][idx])
+            held_at = (lax.shift_right_logical(n, 5), lax.bitwise_and(lax.shift_right_logical(n, 3), 3),
+                       lax.bitwise_and(lax.shift_right_logical(n, 1), 3))
+            keys, vals = [gref[p][(lax.bitwise_and(n, 1),) + tuple(held_at[ORDERS[p % 3][i]] for i in (2, 0, 1))]
+                          for p in (2 * c, 2 * c + 1)]
+            place_keys(c * CK + 16 * b, 16, keys, vals)
         turn(c * CK, CK)
 
     place_keys(PK, ROWS, rkv_ref[:, 0:D], rkv_ref[:, D:])
     turn(PK, ROWS)
     q_in.wait()
     heads_loop(0, HEADS, prepare)
+    for k in range(3):
+        gather.wait(k, 0)
+        gather.start(k, 1)
+    heads_loop(0, 4, first)
+    for k in range(3):
+        gather.wait(k, 1)
     for n in range(8):
-        gather.wait(n, 0)
-        gather.start(n, 1)
-    heads_loop(0, 4, first)
-    for n in range(8):
-        gather.wait(n, 1)
-        gather.start(n, 2)
+        gather.start_last(n)
     heads_loop(4, HEADS, first)
 
     def pass_on(c):
         for n in (2 * c, 2 * c + 1):
-            gather.wait(n, 2)
+            gather.wait("part", n)
             gather.start_core(n)
 
     pass_on(0)
@@ -323,31 +343,58 @@
     for c in range(CHUNKS):
         dk[...] = jnp.zeros_like(dk)
         dv[...] = jnp.zeros_like(dv)
-        staged(lambda h: slope(h, c * CK, CK, 0), lambda h, dp: back(h, dp[...], c * CK, CK, 0, c + 1, 0), (p0, p1))
+        middle = None
+        if c:
+            scatter.ready(c - 1, 0)
+            middle = lambda: scatter.stage(c - 1, 0)
+        staged(lambda h: slope(h, c * CK, CK, 0), lambda h, dp: back(h, dp[...], c * CK, CK, 0, c + 1, 0), (p0, p1), middle)
         own[c][:, 0:16, :] = (dk[...] * SCALE).astype(bf16).reshape(BLOCKS, 16, D)
         own[c][:, 16:, :] = dv[...].astype(bf16).reshape(BLOCKS, 16, D)
         scatter.swap(c)
-        for s in range(c):
-            scatter.stage(c - 1 - s, s)
+        if c >= 2:
+            scatter.stage(c - 2, 1)
+    scatter.stage(0, 2)
     dk[...] = jnp.zeros_like(dk)
     dv[...] = jnp.zeros_like(dv)
 
     def last(h):
         back(h, slope(h, PK, HALF, 0), PK, HALF, 0, 0, 0)
         back(h, slope(h, PK + HALF, HALF, HALF), PK + HALF, HALF, HALF, 0, HALF)
-        dq_ref[:, cols(h)] = (dqt[h] * SCALE).astype(bf16).T
+
+    def rows_out(h):
+        dq_ref[:HALF, cols(h)] = (mm(kt[:, :PK + HALF], e_all[h, :PK + HALF, :HALF]) * SCALE).astype(bf16).T
+        dq_ref[HALF:, cols(h)] = (mm(kt[...], e_all[h, :, HALF:]) * SCALE).astype(bf16).T
+        o_ref[:, cols(h)] = ot[h].astype(bf16).T
+
+    def send_home(src, dst, i):
+        c = pltpu.make_async_copy(src, dst, local.at[i])
+        c.start()
+        return c
 
     heads_loop(0, 4, last)
-    for s in range(4):
-        scatter.stage(3 - s, s)
+    scatter.stage(3, 0)
+    scatter.stage(2, 1)
+    scatter.stage(1, 2)
+    scatter.stage(0, 3)
     heads_loop(4, HEADS, last)
-    for s in range(1, 4):
-        scatter.stage(4 - s, s)
     drkv_ref[:, 0:D] = (dk[...] * SCALE).astype(bf16)
     drkv_ref[:, D:] = dv[...].astype(bf16)
+    home = [send_home(drkv_ref, drkv_hbm, 2)]
+    heads_loop(0, 4, rows_out)
+    half = HEADS * D // 2
+    home.append(send_home(o_ref.at[:, :half], o_hbm.at[:, :half], 3))
+    home.append(send_home(dq_ref.at[:, :half], dq_hbm.at[:, :half], 4))
+    scatter.stage(2, 2)
+    scatter.stage(1, 3)
+    scatter.stage(3, 1)
+    heads_loop(4, HEADS, rows_out)
+    home.append(send_home(o_ref.at[:, half:], o_hbm.at[:, half:], 5))
+    home.append(send_home(dq_ref.at[:, half:], dq_hbm.at[:, half:], 6))
+    scatter.stage(2, 3)
     scatter.stage(3, 2)
-    scatter.stage(2, 3)
     scatter.stage(3, 3)
+    for c in home:
+        c.wait()
     go.drain()
 
 
@@ -361,27 +408,64 @@
     sm = pl.BlockSpec(memory_space=pltpu.SMEM)
     vm = pl.BlockSpec(memory_space=pltpu.VMEM)
     hbm = pl.BlockSpec(memory_space=pl.ANY)
-    sems = 8 * 10 + 8 * 9 + 4
-    return pl.pallas_call(
+    sems = 18 + 8 * 4 + 8 * 9 + 4
+    outs = pl.pallas_call(
         kernel,
         out_shape=(jax.ShapeDtypeStruct(queries.shape, bf16), jax.ShapeDtypeStruct(queries.shape, bf16),
                    jax.ShapeDtypeStruct(resp_kv.shape, bf16), jax.ShapeDtypeStruct((64, 256), f32)),
         in_specs=[sm] * 4 + [hbm] * 2 + [vm] * 2,
-        out_specs=(vm,) * 4,
+        out_specs=(hbm,) * 3 + (vm,),
         scratch_shapes=[pltpu.VMEM((2, SIDE, SIDE, SIDE, 16, D), bf16)] * 8
+        + [pltpu.VMEM((SIDE, SIDE, k, 16, D), bf16) for k in (3, 3, 2)]
         + [pltpu.VMEM((BLOCKS, 32, D), bf16)] * 8 + [pltpu.VMEM((SIDE, SIDE, SIDE, 32, D), bf16)] * 4 + bufs
         + [pltpu.VMEM((ROWS, HEADS * D), bf16), pltpu.VMEM((ROWS, HEADS * D), bf16),
            pltpu.VMEM((NK, 2 * D), bf16), pltpu.VMEM((NK, 2 * D), bf16), pltpu.VMEM((D, NK), bf16),
            pltpu.VMEM((D, NK), bf16), pltpu.VMEM((HEADS, 2 * D, ROWS), bf16), pltpu.VMEM((HEADS, 2 * D, ROWS), bf16),
            pltpu.VMEM((HEADS, ROWS, D), bf16), pltpu.VMEM((HEADS, NK, ROWS), bf16),
            pltpu.VMEM((CHUNKS + 1, HEADS, 1, ROWS), f32), pltpu.VMEM((HEADS, 1, ROWS), f32),
-           pltpu.VMEM((HEADS, D, ROWS), f32), pltpu.VMEM((HEADS, D, ROWS), f32),
+           pltpu.VMEM((HEADS, D, ROWS), f32), pltpu.VMEM((ROWS, HEADS * D), bf16), pltpu.VMEM((ROWS, HEADS * D), bf16),
+           pltpu.VMEM((ROWS, 2 * D), bf16),
            pltpu.VMEM((ROWS, D), f32), pltpu.VMEM((ROWS, D), f32),
            pltpu.VMEM((CK, ROWS), f32), pltpu.VMEM((CK, ROWS), f32), pltpu.VMEM((CK, ROWS), bf16), pltpu.VMEM((CK, ROWS), bf16),
-           pltpu.SemaphoreType.DMA((sems,)), pltpu.SemaphoreType.DMA((sems,)), pltpu.SemaphoreType.DMA((2,))],
+           pltpu.SemaphoreType.DMA((sems,)), pltpu.SemaphoreType.DMA((sems,)), pltpu.SemaphoreType.DMA((7,))],
         compiler_params=pltpu.CompilerParams(collective_id=0, has_side_effects=True, vmem_limit_bytes=62 * 2**20),
         name="shared",
     )(loc, held_block, resp_prompt, resp_len, queries, grad_out, resp_kv, prefix_kv)
+    return deliver(outs)
+
+
+def deliver_kernel(*refs):
+    n = len(refs) // 3
+    sems = refs[-1]
+    moves = []
+    for i in range(n):
+        src, dst, held = refs[i], refs[n + i], refs[2 * n + i]
+        pieces = 4 if i < 2 else 1
+        size = src.shape[0] // pieces
+        for p in range(pieces):
+            rows, k = slice(p * size, p * size + size), len(moves)
+            moves.append((pltpu.make_async_copy(src.at[rows], held.at[rows], sems.at[0, k]),
+                          pltpu.make_async_copy(held.at[rows], dst.at[rows], sems.at[1, k])))
+    for bring, _ in moves:
+        bring.start()
+    for bring, leave in moves:
+        bring.wait()
+        leave.start()
+    for _, leave in moves:
+        leave.wait()
+
+
+def deliver(arrays):
+    hbm = pl.BlockSpec(memory_space=pl.ANY)
+    return pl.pallas_call(
+        deliver_kernel,
+        out_shape=tuple(jax.ShapeDtypeStruct(a.shape, a.dtype) for a in arrays),
+        in_specs=[hbm] * len(arrays),
+        out_specs=(hbm,) * len(arrays),
+        scratch_shapes=[pltpu.VMEM(a.shape, a.dtype) for a in arrays] + [pltpu.SemaphoreType.DMA((2, 10))],
+        compiler_params=pltpu.CompilerParams(vmem_limit_bytes=62 * 2**20),
+        name="deliver",
+    )(*arrays)
 
 
 def solution(mesh):

time: 85.1 us -> 80.3 us (0.944)
  local copies, waits for them, and re-layouts: 4.94 us -> 0 us
    unnamed x10 -> x0, local copies, waits for them, and re-layouts: 4.94 us -> none
    pallas_call x0 -> x1, Pallas kernels: none -> 2.53 us  [deliver(): pl.pallas_call(deliver_kernel, out_shape=tuple((jax.ShapeDtypeStruct(a.sh...]
    pallas_call x1, Pallas kernels: 78 us -> 75.5 us  [on_device(): pl.pallas_call(kernel, out_shape=(jax.ShapeDtypeStruct(queries.shape, bf1...]
where the time goes in v3:
time: 80.3 us; the launch traced here: 80.1 us
  Pallas kernels  78 us (97%)
  other arithmetic  1.28 us (2%)
  between operations  0.82 us (1%)
    pallas_call x1, Pallas kernels, on_device(): pl.pallas_call(kernel, out_shape=(jax.ShapeDtypeStruct(queries.shape, bf1...  75.5 us
    pallas_call x1, Pallas kernels, deliver(): pl.pallas_call(deliver_kernel, out_shape=tuple((jax.ShapeDtypeStruct(a.sh...  2.53 us

profile of v3, /device:TPU:0, one launch (start us, length us, event | category | flops | bytes accessed | tf_op | source)
XLA Modules:
  0.0 80.1 jit_solution(5688860041898390533)
XLA Ops:
  0.6 1.3 %select_reduce_fusion.loc_ref = s32[128]{0:T(128)} fusion(s32[128]{0:T(128)} %held_ref.1), kind=kLoop, calls=%fused_computation | loop fusion | flops 49024 | bytes 1024 | tf_op jit(solution)/shard_map/reduce_sum | solution.py:403
  1.9 75.5 %shared.1 = (bf16[512,1024]{1,0:T(8,128)(2,1)}, bf16[512,1024]{1,0:T(8,128)(2,1)}, bf16[512,256]{1,0:T(8,128)(2,1)}, f32[64,256]{1,0:T(8,128)}) custom-call(s32[128]{0:T(128)} %select_reduce_fusion.loc_ref, s32[128]{0:T(128)} %held_ref.1, s32[128]{0:T(128)} %prompt_ref.1, s32[128]{0:T(128)} %len_ref.1, bf16[512,1024]{1,0:T(8,128)(2,1)} %q_hbm.1, ...), custom_call_target="tpu_custom_call" | custom-call | tf_op jit(solution)/shard_map/shared/pallas_call | solution.py:412
  77.4 2.5 %deliver.1 = (bf16[512,1024]{1,0:T(8,128)(2,1)}, bf16[512,1024]{1,0:T(8,128)(2,1)}, bf16[512,256]{1,0:T(8,128)(2,1)}, f32[64,256]{1,0:T(8,128)}) custom-call(bf16[512,1024]{1,0:T(8,128)(2,1)} %get-tuple-element.8.refs_0_, bf16[512,1024]{1,0:T(8,128)(2,1)} %get-tuple-element.9.refs_1_, bf16[512,256]{1,0:T(8,128)(2,1)} %get-tuple-element.10.refs_2_, ...), custom_call_target="tpu_custom_call" | custom-call | tf_op jit(solution)/shard_map/deliver/pallas_call | solution.py:460

commit v4 on v3

--- a/solution.py
+++ b/solution.py
@@ -92,9 +92,16 @@
         for c in self.flying[key]:
             c.wait_recv()
 
-    def start_core(self, n):
-        v = self.refs[n].at[self.core]
-        self.flying["core", n] = [self.go(v, v, device(self.at, 1 - self.core))]
+    def pass_on(self, n):
+        p, to = self.at[ORDERS[n % 3][2]], device(self.at, 1 - self.core)
+        self.flying["core", n] = []
+        for near in (None, 1, 2, 0):
+            k = p
+            if near is not None:
+                self.flying["part", n][near].wait_recv()
+                k = (p + SIDE - HOPS[near]) % SIDE
+            v = self.refs[n].at[self.core, k]
+            self.flying["core", n].append(self.go(v, v, to))
 
 
 class Scatter:
@@ -168,10 +175,10 @@
                 self.start(c, s)
 
 
-def kernel(loc_ref, held_ref, prompt_ref, len_ref, q_hbm, g_hbm, rkv_ref, x_ref, o_hbm, dq_hbm, drkv_hbm, out_ref, *rest):
+def kernel(held_vec, held_ref, prompt_ref, len_ref, q_hbm, g_hbm, rkv_ref, x_ref, o_hbm, dq_hbm, drkv_hbm, out_ref, *rest):
     gref, stages, rest = rest[:8], rest[8:11], rest[11:]
     own, peer, w, bufs, rest = rest[:4], rest[4:8], rest[8:12], rest[12:36], rest[36:]
-    q_ref, g_ref, kk, vv, kt, vt, q2t, g2t, gp, e_all, ms, ls, ot, o_ref, dq_ref, drkv_ref, dk, dv, s0, s1, p0, p1, send, recv, local = rest
+    q_ref, g_ref, kk, vv, kt, vt, q2t, g2t, gp, e_all, loc_ref, ms, ls, ot, o_ref, dq_ref, drkv_ref, dk, dv, s0, s1, p0, p1, send, recv, local = rest
     at, core = place()
     me = device(at, core)
     barrier = pltpu.get_barrier_semaphore()
@@ -201,12 +208,10 @@
             return 0
         lax.fori_loop(lo // step, hi // step, body, 0)
 
-    def staged(ahead, item, slots, middle=None):
+    def staged(ahead, item, slots):
         slots[0][...] = ahead(0)
 
         def body(i, _):
-            if middle is not None:
-                pl.when(i == 1)(middle)
             for u in range(UNROLL):
                 h = i * UNROLL + u
                 slots[(u + 1) % 2][...] = ahead(lax.rem(h + 1, HEADS))
@@ -214,7 +219,19 @@
             return 0
         lax.fori_loop(0, HEADS // UNROLL, body, 0)
 
+    def straight(ahead, item, slots, middle):
+        slots[0][...] = ahead(0)
+        for h in range(HEADS):
+            if h == HEADS // 2:
+                for job in middle:
+                    scatter.stage(*job)
+            if h + 1 < HEADS:
+                slots[(h + 1) % 2][...] = ahead(h + 1)
+            item(h, slots[h % 2])
+
     def cols(h):
+        if isinstance(h, int):
+            return slice(h * D, h * D + D)
         return pl.ds(pl.multiple_of(h * D, D), D)
 
     def prepare(h):
@@ -223,6 +240,8 @@
         lo = (qs - hi.astype(f32)).astype(bf16)
         q2t[h, 0:D] = hi.T
         q2t[h, D:] = lo.T
+        g2t[h, 0:D] = g_ref[:, cols(h)].T
+        g2t[h, D + 16:] = jnp.zeros((D - 16, ROWS), bf16)
 
     def place_keys(k0, kn, keys, vals):
         kk[k0:k0 + kn, 0:D] = keys
@@ -275,7 +294,7 @@
         f = jnp.where(live, 1.0 / ls[h], 0.0)
         o = ot[h] * f
         ot[h] = o
-        gt = g_ref[:, cols(h)].T.astype(f32)
+        gt = g2t[h, 0:D].astype(f32)
         gt = jnp.where(live, gt, 0.0) * f
         neg = -jnp.sum(gt * o, axis=0, keepdims=True)
         gb = gt.astype(bf16)
@@ -285,7 +304,6 @@
         extra = jnp.where(sub == 0, hi, jnp.where(sub == 1, neg - hi, 0.0)).astype(bf16)
         g2t[h, 0:D] = gb
         g2t[h, D:D + 16] = extra
-        g2t[h, D + 16:] = jnp.zeros((D - 16, ROWS), bf16)
 
     def slope(h, k0, kn, r0):
         return mm(vv[k0:k0 + kn, :], g2t[h, :, r0:]).astype(bf16)
@@ -301,9 +319,8 @@
     def load_chunk(c):
         for n in (2 * c, 2 * c + 1):
             gather.wait("core", n)
-        prompt = prompt_ref[me]
         for b in range(BLOCKS):
-            n = loc_ref[prompt * BLOCKS + b]
+            n = loc_ref[b]
             held_at = (lax.shift_right_logical(n, 5), lax.bitwise_and(lax.shift_right_logical(n, 3), 3),
                        lax.bitwise_and(lax.shift_right_logical(n, 1), 3))
             keys, vals = [gref[p][(lax.bitwise_and(n, 1),) + tuple(held_at[ORDERS[p % 3][i]] for i in (2, 0, 1))]
@@ -314,6 +331,7 @@
     place_keys(PK, ROWS, rkv_ref[:, 0:D], rkv_ref[:, D:])
     turn(PK, ROWS)
     q_in.wait()
+    g_in.wait()
     heads_loop(0, HEADS, prepare)
     for k in range(3):
         gather.wait(k, 0)
@@ -325,10 +343,15 @@
         gather.start_last(n)
     heads_loop(4, HEADS, first)
 
+    lane = lax.broadcasted_iota(jnp.int32, (1, 128), 1)
+    held_row = held_vec[...].reshape(1, 128)
+    base = prompt_ref[me] * BLOCKS
+    for b in range(BLOCKS):
+        loc_ref[b] = jnp.max(jnp.where(held_row == base + b, lane, 0))
+
     def pass_on(c):
         for n in (2 * c, 2 * c + 1):
-            gather.wait("part", n)
-            gather.start_core(n)
+            gather.pass_on(n)
 
     pass_on(0)
     for c in range(CHUNKS):
@@ -336,24 +359,17 @@
         if c + 1 < CHUNKS:
             pass_on(c + 1)
         forward(c)
-    g_in.wait()
     heads_loop(0, HEADS, finish)
 
     scatter = Scatter(go, at, core, held_ref, prompt_ref, own, peer, w, bufs, out_ref)
     for c in range(CHUNKS):
         dk[...] = jnp.zeros_like(dk)
         dv[...] = jnp.zeros_like(dv)
-        middle = None
-        if c:
-            scatter.ready(c - 1, 0)
-            middle = lambda: scatter.stage(c - 1, 0)
-        staged(lambda h: slope(h, c * CK, CK, 0), lambda h, dp: back(h, dp[...], c * CK, CK, 0, c + 1, 0), (p0, p1), middle)
+        middle = [] if c == 0 else [(c - 1, 0)] if c < 3 else [(2, 0), (0, 1)]
+        straight(lambda h: slope(h, c * CK, CK, 0), lambda h, dp: back(h, dp[...], c * CK, CK, 0, c + 1, 0), (p0, p1), middle)
         own[c][:, 0:16, :] = (dk[...] * SCALE).astype(bf16).reshape(BLOCKS, 16, D)
         own[c][:, 16:, :] = dv[...].astype(bf16).reshape(BLOCKS, 16, D)
         scatter.swap(c)
-        if c >= 2:
-            scatter.stage(c - 2, 1)
-    scatter.stage(0, 2)
     dk[...] = jnp.zeros_like(dk)
     dv[...] = jnp.zeros_like(dv)
 
@@ -371,12 +387,15 @@
         c.start()
         return c
 
-    heads_loop(0, 4, last)
+    heads_loop(0, 2, last, 2)
     scatter.stage(3, 0)
+    scatter.stage(1, 1)
+    scatter.stage(0, 2)
+    heads_loop(2, 4, last, 2)
+    heads_loop(4, HEADS, last)
     scatter.stage(2, 1)
     scatter.stage(1, 2)
     scatter.stage(0, 3)
-    heads_loop(4, HEADS, last)
     drkv_ref[:, 0:D] = (dk[...] * SCALE).astype(bf16)
     drkv_ref[:, D:] = dv[...].astype(bf16)
     home = [send_home(drkv_ref, drkv_hbm, 2)]
@@ -384,9 +403,9 @@
     half = HEADS * D // 2
     home.append(send_home(o_ref.at[:, :half], o_hbm.at[:, :half], 3))
     home.append(send_home(dq_ref.at[:, :half], dq_hbm.at[:, :half], 4))
+    scatter.stage(3, 1)
     scatter.stage(2, 2)
     scatter.stage(1, 3)
-    scatter.stage(3, 1)
     heads_loop(4, HEADS, rows_out)
     home.append(send_home(o_ref.at[:, half:], o_hbm.at[:, half:], 5))
     home.append(send_home(dq_ref.at[:, half:], dq_hbm.at[:, half:], 6))
@@ -399,8 +418,6 @@
 
 
 def on_device(queries, resp_kv, prefix_kv, grad_out, held_block, resp_prompt, resp_len):
-    spots = jnp.arange(128, dtype=jnp.int32)
-    loc = jnp.sum(jnp.where(held_block[None, :] == spots[:, None], spots[None, :], 0), axis=1).astype(jnp.int32)
     bufs = []
     for n in range(8):
         for i in range(3):
@@ -408,12 +425,12 @@
     sm = pl.BlockSpec(memory_space=pltpu.SMEM)
     vm = pl.BlockSpec(memory_space=pltpu.VMEM)
     hbm = pl.BlockSpec(memory_space=pl.ANY)
-    sems = 18 + 8 * 4 + 8 * 9 + 4
+    sems = 18 + 8 * 7 + 8 * 9 + 4
     outs = pl.pallas_call(
         kernel,
         out_shape=(jax.ShapeDtypeStruct(queries.shape, bf16), jax.ShapeDtypeStruct(queries.shape, bf16),
                    jax.ShapeDtypeStruct(resp_kv.shape, bf16), jax.ShapeDtypeStruct((64, 256), f32)),
-        in_specs=[sm] * 4 + [hbm] * 2 + [vm] * 2,
+        in_specs=[vm] + [sm] * 3 + [hbm] * 2 + [vm] * 2,
         out_specs=(hbm,) * 3 + (vm,),
         scratch_shapes=[pltpu.VMEM((2, SIDE, SIDE, SIDE, 16, D), bf16)] * 8
         + [pltpu.VMEM((SIDE, SIDE, k, 16, D), bf16) for k in (3, 3, 2)]
@@ -422,6 +439,7 @@
            pltpu.VMEM((NK, 2 * D), bf16), pltpu.VMEM((NK, 2 * D), bf16), pltpu.VMEM((D, NK), bf16),
            pltpu.VMEM((D, NK), bf16), pltpu.VMEM((HEADS, 2 * D, ROWS), bf16), pltpu.VMEM((HEADS, 2 * D, ROWS), bf16),
            pltpu.VMEM((HEADS, ROWS, D), bf16), pltpu.VMEM((HEADS, NK, ROWS), bf16),
+           pltpu.SMEM((BLOCKS,), jnp.int32),
            pltpu.VMEM((CHUNKS + 1, HEADS, 1, ROWS), f32), pltpu.VMEM((HEADS, 1, ROWS), f32),
            pltpu.VMEM((HEADS, D, ROWS), f32), pltpu.VMEM((ROWS, HEADS * D), bf16), pltpu.VMEM((ROWS, HEADS * D), bf16),
            pltpu.VMEM((ROWS, 2 * D), bf16),
@@ -430,7 +448,7 @@
            pltpu.SemaphoreType.DMA((sems,)), pltpu.SemaphoreType.DMA((sems,)), pltpu.SemaphoreType.DMA((7,))],
         compiler_params=pltpu.CompilerParams(collective_id=0, has_side_effects=True, vmem_limit_bytes=62 * 2**20),
         name="shared",
-    )(loc, held_block, resp_prompt, resp_len, queries, grad_out, resp_kv, prefix_kv)
+    )(held_block, held_block, resp_prompt, resp_len, queries, grad_out, resp_kv, prefix_kv)
     return deliver(outs)
 
 

time: 80.3 us -> 79.6 us (level)
  other arithmetic: 1.28 us -> 0 us
    reduce_sum x1 -> x0, other arithmetic: 1.28 us -> none  [on_device(): jnp.sum(jnp.where(held_block[None, :] == spots[:, None], spots[None, :],...]
where the time goes in v4:
time: 79.6 us; the launch traced here: 79.5 us
  Pallas kernels  78.7 us (99%)
  between operations  0.82 us (1%)
    pallas_call x1, Pallas kernels, on_device(): pl.pallas_call(kernel, out_shape=(jax.ShapeDtypeStruct(queries.shape, bf1...  76.1 us
    pallas_call x1, Pallas kernels, deliver(): pl.pallas_call(deliver_kernel, out_shape=tuple((jax.ShapeDtypeStruct(a.sh...  2.53 us

profile of v4, /device:TPU:0, one launch (start us, length us, event | category | flops | bytes accessed | tf_op | source)
XLA Modules:
  0.0 79.5 jit_solution(11265560676275551606)
XLA Ops:
  0.6 76.1 %shared.1 = (bf16[512,1024]{1,0:T(8,128)(2,1)}, bf16[512,1024]{1,0:T(8,128)(2,1)}, bf16[512,256]{1,0:T(8,128)(2,1)}, f32[64,256]{1,0:T(8,128)}) custom-call(s32[128]{0:T(128)} %held_ref.1, s32[128]{0:T(128)} %held_ref.1, s32[128]{0:T(128)} %prompt_ref.1, s32[128]{0:T(128)} %len_ref.1, bf16[512,1024]{1,0:T(8,128)(2,1)} %q_hbm.1, bf16[512,1024]{1,0:T(8,128)(2,1)} %g_hbm.1, ...), custom_call_target="tpu_custom_call" | custom-call | tf_op jit(solution)/shard_map/shared/pallas_call | solution.py:429
  76.8 2.5 %deliver.1 = (bf16[512,1024]{1,0:T(8,128)(2,1)}, bf16[512,1024]{1,0:T(8,128)(2,1)}, bf16[512,256]{1,0:T(8,128)(2,1)}, f32[64,256]{1,0:T(8,128)}) custom-call(bf16[512,1024]{1,0:T(8,128)(2,1)} %get-tuple-element.8.refs_0_, bf16[512,1024]{1,0:T(8,128)(2,1)} %get-tuple-element.9.refs_1_, bf16[512,256]{1,0:T(8,128)(2,1)} %get-tuple-element.10.refs_2_, ...), custom_call_target="tpu_custom_call" | custom-call | tf_op jit(solution)/shard_map/deliver/pallas_call | solution.py:478

commit v5 on v4

--- a/solution.py
+++ b/solution.py
@@ -75,18 +75,18 @@
     def put(self, x_ref):
         for n, (c, t) in enumerate(PARTS):
             a, b, _ = ORDERS[n % 3]
-            self.stages[n % 3][self.at[a], self.at[b], n // 3] = x_ref[16 * c:16 * c + 16, D * t:D * t + D]
+            self.stages[n % 3][n // 3, self.at[b], self.at[a]] = x_ref[16 * c:16 * c + 16, D * t:D * t + D]
 
     def start(self, k, i):
         a, b, _ = ORDERS[k]
-        v = self.stages[k].at[self.at[a], self.at[b]] if i == 0 else self.stages[k].at[:, self.at[b]]
+        v = self.stages[k].at[:, self.at[b], self.at[a]] if i == 0 else self.stages[k].at[:, self.at[b]]
         self.flying[k, i] = [self.go(v, v, device(moved(self.at, ORDERS[k][i], s), self.core)) for s in HOPS]
 
     def start_last(self, n):
         a = ORDERS[n % 3][2]
-        src, dst = self.stages[n % 3].at[:, :, n // 3], self.refs[n].at[self.core, self.at[a]]
+        src, dst = self.stages[n % 3].at[n // 3], self.refs[n].at[self.core, self.at[a]]
         self.flying["part", n] = [self.go(src, dst, device(moved(self.at, a, s), self.core)) for s in HOPS]
-        self.refs[n][self.core, self.at[a]] = self.stages[n % 3][:, :, n // 3]
+        self.refs[n][self.core, self.at[a]] = self.stages[n % 3][n // 3]
 
     def wait(self, *key):
         for c in self.flying[key]:
@@ -114,35 +114,35 @@
         self.other_core = device(at, 1 - core)
 
     def swap(self, c):
-        self.flying[c] = self.go(self.own[c], self.peer[c], self.other_core)
+        self.flying[c] = self.go(self.own[c].at[0:BLOCKS], self.peer[c].at[0:BLOCKS], self.other_core)
 
     def fill(self, c):
         self.flying[c].wait_recv()
         mine = self.prompt[device(self.at, self.core)]
         other = self.prompt[device(self.at, 1 - self.core)]
-        own, peer, w = self.own[c], self.peer[c], self.w[c]
-        zero = jnp.zeros((32, D), bf16)
+        own, peer = self.own[c], self.peer[c]
 
         def body(j, _):
-            for u in range(4):
-                b = self.held[(j * 4 + u) * 2 + self.core]
+            for u in range(8):
+                b = self.held[(j * 8 + u) * 2 + self.core]
                 p, k = lax.shift_right_logical(b, 5), lax.bitwise_and(b, 31)
-                w[j // 4, j % 4, u] = jnp.where(p == mine, own[k], zero) + jnp.where(p == other, peer[k], zero)
+                v = own[jnp.where(p == mine, k, BLOCKS)] + peer[jnp.where(p == other, k, BLOCKS)]
+                to = (j // 2, j % 2 * 2 + u // 4, u % 4)
+                for t in range(2):
+                    n = 2 * c + t
+                    self.w[n][tuple(to[a] for a in ORDERS[n % 3])] = v[16 * t:16 * t + 16]
             return 0
 
-        lax.fori_loop(0, 16, body, 0)
+        lax.fori_loop(0, 8, body, 0)
 
     def spot(self, n, i, k):
-        c, t = PARTS[n]
-        order = ORDERS[n % 3]
-        idx = [self.at[a] if a in order[:i] else k if a == order[i] else slice(0, SIDE) for a in range(3)]
-        return (*idx, slice(16 * t, 16 * t + 16), slice(None))
+        return tuple(self.at[a] for a in ORDERS[n % 3][:i]) + (k,)
 
     def ready(self, c, i):
         for n in (2 * c, 2 * c + 1):
             a = ORDERS[n % 3][i]
             self.flying[n, i] = [
-                self.go.ready(self.w[c].at[self.spot(n, i, self.coord[a][j])], self.bufs[3 * n + i].at[j], self.dev[a][j])
+                self.go.ready(self.w[n].at[self.spot(n, i, self.coord[a][j])], self.bufs[3 * n + i].at[j], self.dev[a][j])
                 for j in range(3)]
 
     def start(self, c, i):
@@ -158,9 +158,9 @@
                 f.wait_recv()
             buf = self.bufs[3 * n + i]
             here = self.spot(n, i, self.at[ORDERS[n % 3][i]])
-            total = (self.w[c][here].astype(f32) + buf[0].astype(f32)) + (buf[1].astype(f32) + buf[2].astype(f32))
+            total = (self.w[n][here].astype(f32) + buf[0].astype(f32)) + (buf[1].astype(f32) + buf[2].astype(f32))
             if i < 2:
-                self.w[c][here] = total.astype(bf16)
+                self.w[n][here] = total.astype(bf16)
             else:
                 t = n % 2
                 self.out[16 * c:16 * c + 16, D * t:D * t + D] = total
@@ -177,7 +177,7 @@
 
 def kernel(held_vec, held_ref, prompt_ref, len_ref, q_hbm, g_hbm, rkv_ref, x_ref, o_hbm, dq_hbm, drkv_hbm, out_ref, *rest):
     gref, stages, rest = rest[:8], rest[8:11], rest[11:]
-    own, peer, w, bufs, rest = rest[:4], rest[4:8], rest[8:12], rest[12:36], rest[36:]
+    own, peer, w, bufs, rest = rest[:4], rest[4:8], rest[8:16], rest[16:40], rest[40:]
     q_ref, g_ref, kk, vv, kt, vt, q2t, g2t, gp, e_all, loc_ref, ms, ls, ot, o_ref, dq_ref, drkv_ref, dk, dv, s0, s1, p0, p1, send, recv, local = rest
     at, core = place()
     me = device(at, core)
@@ -196,6 +196,8 @@
     for k in range(3):
         gather.start(k, 0)
 
+    for ref in (*own, *peer):
+        ref[BLOCKS] = jnp.zeros((32, D), bf16)
     length = len_ref[me]
     live = lax.broadcasted_iota(jnp.int32, (1, ROWS), 1) < length
     tri = lax.broadcasted_iota(jnp.int32, (HALF, HALF), 0) <= lax.broadcasted_iota(jnp.int32, (HALF, HALF), 1)
@@ -323,7 +325,7 @@
             n = loc_ref[b]
             held_at = (lax.shift_right_logical(n, 5), lax.bitwise_and(lax.shift_right_logical(n, 3), 3),
                        lax.bitwise_and(lax.shift_right_logical(n, 1), 3))
-            keys, vals = [gref[p][(lax.bitwise_and(n, 1),) + tuple(held_at[ORDERS[p % 3][i]] for i in (2, 0, 1))]
+            keys, vals = [gref[p][(lax.bitwise_and(n, 1),) + tuple(held_at[ORDERS[p % 3][i]] for i in (2, 1, 0))]
                           for p in (2 * c, 2 * c + 1)]
             place_keys(c * CK + 16 * b, 16, keys, vals)
         turn(c * CK, CK)
@@ -367,8 +369,8 @@
         dv[...] = jnp.zeros_like(dv)
         middle = [] if c == 0 else [(c - 1, 0)] if c < 3 else [(2, 0), (0, 1)]
         straight(lambda h: slope(h, c * CK, CK, 0), lambda h, dp: back(h, dp[...], c * CK, CK, 0, c + 1, 0), (p0, p1), middle)
-        own[c][:, 0:16, :] = (dk[...] * SCALE).astype(bf16).reshape(BLOCKS, 16, D)
-        own[c][:, 16:, :] = dv[...].astype(bf16).reshape(BLOCKS, 16, D)
+        own[c][0:BLOCKS, 0:16, :] = (dk[...] * SCALE).astype(bf16).reshape(BLOCKS, 16, D)
+        own[c][0:BLOCKS, 16:, :] = dv[...].astype(bf16).reshape(BLOCKS, 16, D)
         scatter.swap(c)
     dk[...] = jnp.zeros_like(dk)
     dv[...] = jnp.zeros_like(dv)
@@ -433,8 +435,8 @@
         in_specs=[vm] + [sm] * 3 + [hbm] * 2 + [vm] * 2,
         out_specs=(hbm,) * 3 + (vm,),
         scratch_shapes=[pltpu.VMEM((2, SIDE, SIDE, SIDE, 16, D), bf16)] * 8
-        + [pltpu.VMEM((SIDE, SIDE, k, 16, D), bf16) for k in (3, 3, 2)]
-        + [pltpu.VMEM((BLOCKS, 32, D), bf16)] * 8 + [pltpu.VMEM((SIDE, SIDE, SIDE, 32, D), bf16)] * 4 + bufs
+        + [pltpu.VMEM((k, SIDE, SIDE, 16, D), bf16) for k in (3, 3, 2)]
+        + [pltpu.VMEM((BLOCKS + 1, 32, D), bf16)] * 8 + [pltpu.VMEM((SIDE, SIDE, SIDE, 16, D), bf16)] * 8 + bufs
         + [pltpu.VMEM((ROWS, HEADS * D), bf16), pltpu.VMEM((ROWS, HEADS * D), bf16),
            pltpu.VMEM((NK, 2 * D), bf16), pltpu.VMEM((NK, 2 * D), bf16), pltpu.VMEM((D, NK), bf16),
            pltpu.VMEM((D, NK), bf16), pltpu.VMEM((HEADS, 2 * D, ROWS), bf16), pltpu.VMEM((HEADS, 2 * D, ROWS), bf16),

time: 79.6 us -> 79.3 us (level)
  no operation moved by 1% of the time
where the time goes in v5:
time: 79.3 us; the launch traced here: 79.1 us
  Pallas kernels  78.3 us (99%)
  between operations  0.82 us (1%)
    pallas_call x1, Pallas kernels, on_device(): pl.pallas_call(kernel, out_shape=(jax.ShapeDtypeStruct(queries.shape, bf1...  75.8 us
    pallas_call x1, Pallas kernels, deliver(): pl.pallas_call(deliver_kernel, out_shape=tuple((jax.ShapeDtypeStruct(a.sh...  2.53 us

profile of v5, /device:TPU:0, one launch (start us, length us, event | category | flops | bytes accessed | tf_op | source)
XLA Modules:
  0.0 79.1 jit_solution(15897483144879919810)
XLA Ops:
  0.6 75.8 %shared.1 = (bf16[512,1024]{1,0:T(8,128)(2,1)}, bf16[512,1024]{1,0:T(8,128)(2,1)}, bf16[512,256]{1,0:T(8,128)(2,1)}, f32[64,256]{1,0:T(8,128)}) custom-call(s32[128]{0:T(128)} %held_ref.1, s32[128]{0:T(128)} %held_ref.1, s32[128]{0:T(128)} %prompt_ref.1, s32[128]{0:T(128)} %len_ref.1, bf16[512,1024]{1,0:T(8,128)(2,1)} %q_hbm.1, bf16[512,1024]{1,0:T(8,128)(2,1)} %g_hbm.1, ...), custom_call_target="tpu_custom_call" | custom-call | tf_op jit(solution)/shard_map/shared/pallas_call | solution.py:431
  76.4 2.5 %deliver.1 = (bf16[512,1024]{1,0:T(8,128)(2,1)}, bf16[512,1024]{1,0:T(8,128)(2,1)}, bf16[512,256]{1,0:T(8,128)(2,1)}, f32[64,256]{1,0:T(8,128)}) custom-call(bf16[512,1024]{1,0:T(8,128)(2,1)} %get-tuple-element.8.refs_0_, bf16[512,1024]{1,0:T(8,128)(2,1)} %get-tuple-element.9.refs_1_, bf16[512,256]{1,0:T(8,128)(2,1)} %get-tuple-element.10.refs_2_, ...), custom_call_target="tpu_custom_call" | custom-call | tf_op jit(solution)/shard_map/deliver/pallas_call | solution.py:480

commit v6 on v5

--- a/solution.py
+++ b/solution.py
@@ -210,26 +210,25 @@
             return 0
         lax.fori_loop(lo // step, hi // step, body, 0)
 
-    def staged(ahead, item, slots):
+    def staged(ahead, item, slots, middle=()):
         slots[0][...] = ahead(0)
 
+        for job in middle:
+            scatter.ready(*job)
+
+        def between():
+            for job in middle:
+                scatter.stage(*job)
+
         def body(i, _):
+            if middle:
+                pl.when(i == 1)(between)
             for u in range(UNROLL):
                 h = i * UNROLL + u
                 slots[(u + 1) % 2][...] = ahead(lax.rem(h + 1, HEADS))
                 item(h, slots[u % 2])
             return 0
         lax.fori_loop(0, HEADS // UNROLL, body, 0)
-
-    def straight(ahead, item, slots, middle):
-        slots[0][...] = ahead(0)
-        for h in range(HEADS):
-            if h == HEADS // 2:
-                for job in middle:
-                    scatter.stage(*job)
-            if h + 1 < HEADS:
-                slots[(h + 1) % 2][...] = ahead(h + 1)
-            item(h, slots[h % 2])
 
     def cols(h):
         if isinstance(h, int):
@@ -368,7 +367,7 @@
         dk[...] = jnp.zeros_like(dk)
         dv[...] = jnp.zeros_like(dv)
         middle = [] if c == 0 else [(c - 1, 0)] if c < 3 else [(2, 0), (0, 1)]
-        straight(lambda h: slope(h, c * CK, CK, 0), lambda h, dp: back(h, dp[...], c * CK, CK, 0, c + 1, 0), (p0, p1), middle)
+        staged(lambda h: slope(h, c * CK, CK, 0), lambda h, dp: back(h, dp[...], c * CK, CK, 0, c + 1, 0), (p0, p1), middle)
         own[c][0:BLOCKS, 0:16, :] = (dk[...] * SCALE).astype(bf16).reshape(BLOCKS, 16, D)
         own[c][0:BLOCKS, 16:, :] = dv[...].astype(bf16).reshape(BLOCKS, 16, D)
         scatter.swap(c)
@@ -406,13 +405,13 @@
     home.append(send_home(o_ref.at[:, :half], o_hbm.at[:, :half], 3))
     home.append(send_home(dq_ref.at[:, :half], dq_hbm.at[:, :half], 4))
     scatter.stage(3, 1)
-    scatter.stage(2, 2)
-    scatter.stage(1, 3)
     heads_loop(4, HEADS, rows_out)
     home.append(send_home(o_ref.at[:, half:], o_hbm.at[:, half:], 5))
     home.append(send_home(dq_ref.at[:, half:], dq_hbm.at[:, half:], 6))
+    scatter.stage(2, 2)
+    scatter.stage(1, 3)
+    scatter.stage(3, 2)
     scatter.stage(2, 3)
-    scatter.stage(3, 2)
     scatter.stage(3, 3)
     for c in home:
         c.wait()

time: 79.3 us -> 80.1 us (1.010)
    pallas_call x1, Pallas kernels: 75.8 us -> 76.6 us  [on_device(): pl.pallas_call(kernel, out_shape=(jax.ShapeDtypeStruct(queries.shape, bf1...]
where the time goes in v6:
time: 80.1 us; the launch traced here: 80 us
  Pallas kernels  79.1 us (99%)
  between operations  0.82 us (1%)
    pallas_call x1, Pallas kernels, on_device(): pl.pallas_call(kernel, out_shape=(jax.ShapeDtypeStruct(queries.shape, bf1...  76.6 us
    pallas_call x1, Pallas kernels, deliver(): pl.pallas_call(deliver_kernel, out_shape=tuple((jax.ShapeDtypeStruct(a.sh...  2.53 us

profile of v6, /device:TPU:0, one launch (start us, length us, event | category | flops | bytes accessed | tf_op | source)
XLA Modules:
  0.0 80.0 jit_solution(3658619461062103821)
XLA Ops:
  0.6 76.6 %shared.1 = (bf16[512,1024]{1,0:T(8,128)(2,1)}, bf16[512,1024]{1,0:T(8,128)(2,1)}, bf16[512,256]{1,0:T(8,128)(2,1)}, f32[64,256]{1,0:T(8,128)}) custom-call(s32[128]{0:T(128)} %held_ref.1, s32[128]{0:T(128)} %held_ref.1, s32[128]{0:T(128)} %prompt_ref.1, s32[128]{0:T(128)} %len_ref.1, bf16[512,1024]{1,0:T(8,128)(2,1)} %q_hbm.1, bf16[512,1024]{1,0:T(8,128)(2,1)} %g_hbm.1, ...), custom_call_target="tpu_custom_call" | custom-call | tf_op jit(solution)/shard_map/shared/pallas_call | solution.py:430
  77.3 2.5 %deliver.1 = (bf16[512,1024]{1,0:T(8,128)(2,1)}, bf16[512,1024]{1,0:T(8,128)(2,1)}, bf16[512,256]{1,0:T(8,128)(2,1)}, f32[64,256]{1,0:T(8,128)}) custom-call(bf16[512,1024]{1,0:T(8,128)(2,1)} %get-tuple-element.8.refs_0_, bf16[512,1024]{1,0:T(8,128)(2,1)} %get-tuple-element.9.refs_1_, bf16[512,256]{1,0:T(8,128)(2,1)} %get-tuple-element.10.refs_2_, ...), custom_call_target="tpu_custom_call" | custom-call | tf_op jit(solution)/shard_map/deliver/pallas_call | solution.py:479

commit v7 on v5

--- a/solution.py
+++ b/solution.py
@@ -92,16 +92,18 @@
         for c in self.flying[key]:
             c.wait_recv()
 
-    def pass_on(self, n):
+    def ready_core(self, n):
         p, to = self.at[ORDERS[n % 3][2]], device(self.at, 1 - self.core)
         self.flying["core", n] = []
         for near in (None, 1, 2, 0):
-            k = p
+            v = self.refs[n].at[self.core, p if near is None else (p + SIDE - HOPS[near]) % SIDE]
+            self.flying["core", n].append(self.go.ready(v, v, to))
+
+    def pass_on(self, n):
+        for near, c in zip((None, 1, 2, 0), self.flying["core", n]):
             if near is not None:
                 self.flying["part", n][near].wait_recv()
-                k = (p + SIDE - HOPS[near]) % SIDE
-            v = self.refs[n].at[self.core, k]
-            self.flying["core", n].append(self.go(v, v, to))
+            c.start()
 
 
 class Scatter:
@@ -210,10 +212,12 @@
             return 0
         lax.fori_loop(lo // step, hi // step, body, 0)
 
-    def staged(ahead, item, slots):
+    def staged(ahead, item, slots, middle=None):
         slots[0][...] = ahead(0)
 
         def body(i, _):
+            if middle is not None:
+                pl.when(i == 1)(middle)
             for u in range(UNROLL):
                 h = i * UNROLL + u
                 slots[(u + 1) % 2][...] = ahead(lax.rem(h + 1, HEADS))
@@ -274,7 +278,7 @@
         ot[h, :, 0:HALF] = oa[:, :HALF]
         ot[h, :, HALF:] = oa[:, HALF:] + ob
 
-    def forward(c):
+    def forward(c, middle):
         k0 = c * CK
 
         def ahead(h):
@@ -290,7 +294,7 @@
             e_all[h, k0:k0 + CK, :] = e
             ot[h] = ot[h] * fade + mm(vt[:, k0:k0 + CK], e)
             ms[c + 1, h] = m
-        staged(ahead, item, (s0, s1))
+        staged(ahead, item, (s0, s1), middle)
 
     def finish(h):
         f = jnp.where(live, 1.0 / ls[h], 0.0)
@@ -355,12 +359,12 @@
         for n in (2 * c, 2 * c + 1):
             gather.pass_on(n)
 
+    for n in range(8):
+        gather.ready_core(n)
     pass_on(0)
     for c in range(CHUNKS):
         load_chunk(c)
-        if c + 1 < CHUNKS:
-            pass_on(c + 1)
-        forward(c)
+        forward(c, (lambda: pass_on(c + 1)) if c + 1 < CHUNKS else None)
     heads_loop(0, HEADS, finish)
 
     scatter = Scatter(go, at, core, held_ref, prompt_ref, own, peer, w, bufs, out_ref)

time: 79.3 us -> 79.4 us (level)
  no operation moved by 1% of the time
where the time goes in v7:
time: 79.4 us; the launch traced here: 79.2 us
  Pallas kernels  78.4 us (99%)
  between operations  0.82 us (1%)
    pallas_call x1, Pallas kernels, on_device(): pl.pallas_call(kernel, out_shape=(jax.ShapeDtypeStruct(queries.shape, bf1...  75.9 us
    pallas_call x1, Pallas kernels, deliver(): pl.pallas_call(deliver_kernel, out_shape=tuple((jax.ShapeDtypeStruct(a.sh...  2.53 us

profile of v7, /device:TPU:0, one launch (start us, length us, event | category | flops | bytes accessed | tf_op | source)
XLA Modules:
  0.0 79.2 jit_solution(9760108869854689622)
XLA Ops:
  0.6 75.9 %shared.1 = (bf16[512,1024]{1,0:T(8,128)(2,1)}, bf16[512,1024]{1,0:T(8,128)(2,1)}, bf16[512,256]{1,0:T(8,128)(2,1)}, f32[64,256]{1,0:T(8,128)}) custom-call(s32[128]{0:T(128)} %held_ref.1, s32[128]{0:T(128)} %held_ref.1, s32[128]{0:T(128)} %prompt_ref.1, s32[128]{0:T(128)} %len_ref.1, bf16[512,1024]{1,0:T(8,128)(2,1)} %q_hbm.1, bf16[512,1024]{1,0:T(8,128)(2,1)} %g_hbm.1, ...), custom_call_target="tpu_custom_call" | custom-call | tf_op jit(solution)/shard_map/shared/pallas_call | solution.py:435
  76.5 2.5 %deliver.1 = (bf16[512,1024]{1,0:T(8,128)(2,1)}, bf16[512,1024]{1,0:T(8,128)(2,1)}, bf16[512,256]{1,0:T(8,128)(2,1)}, f32[64,256]{1,0:T(8,128)}) custom-call(bf16[512,1024]{1,0:T(8,128)(2,1)} %get-tuple-element.8.refs_0_, bf16[512,1024]{1,0:T(8,128)(2,1)} %get-tuple-element.9.refs_1_, bf16[512,256]{1,0:T(8,128)(2,1)} %get-tuple-element.10.refs_2_, ...), custom_call_target="tpu_custom_call" | custom-call | tf_op jit(solution)/shard_map/deliver/pallas_call | solution.py:484
